TPU v7x, 128 devices: a whole 4x4x4 slice. The times are simulated.
128 devices in a mesh: row: 16 (over x_hi, y, core), col: 8 (over x_lo, z).
Axes of the slice: x: 4 (x_hi: 2, x_lo: 2; x = x_hi * 2 + x_lo), y: 4, z: 4, core: 2. Of those that a mesh axis runs over, the one named last changes fastest.
Arguments:
- multispectral: float32 [8, 512, 1024], P('col', 'row'), may hold values from -6 to 6
- panchromatic: float32 [2048, 4096], P('row', 'col'), may hold values from -6 to 6
- band_gains: float32 [8, 3], replicated, may hold values from 0.5 to 2
Outputs:
- sharpened: float32 [8, 2048, 4096], P(None, 'row', 'col')
All inputs are finite; a program needn't handle non-finite values.
Results may differ from a plain program's by a relative error of at most 0.000065.
Values sent between devices are 32-bit elements; how exact they have to be, the bound alone decides.
A program may use at most 128 MiB of HBM per device.

v0:
```python
import math

import jax
import jax.numpy as jnp
import numpy as np
from jax import lax
from jax.sharding import PartitionSpec as P

LEVELS = 3


daubechies_taps = [
    0.2303778133088964,
    0.7148465705529155,
    0.6308807679298587,
    -0.0279837694168599,
    -0.1870348117190931,
    0.0308413818355607,
    0.0328830116668852,
    -0.010597401785069,
]


def extended_2(cells, sides, width):
    for axis, dim in sides:
        count = lax.axis_size(axis)
        head = lax.slice_in_dim(cells, 0, width, axis=dim)
        tail = lax.slice_in_dim(cells, cells.shape[dim] - width, cells.shape[dim], axis=dim)
        cells = jnp.concatenate(
            [
                lax.ppermute(tail, axis, [(i, (i + 1) % count) for i in range(count)]),
                cells,
                lax.ppermute(head, axis, [((i + 1) % count, i) for i in range(count)]),
            ],
            axis=dim,
        )
    return cells


def tree_filters(tree_index):
    lowpass = list(daubechies_taps) if tree_index == 0 else list(reversed(daubechies_taps))
    highpass = [(-1) ** tap_index * lowpass[7 - tap_index] for tap_index in range(8)]
    return (lowpass, highpass, 3 + tree_index)


def cubic_weight(distance):
    magnitude = abs(distance)
    if magnitude <= 1.0:
        return 1.5 * magnitude**3 - 2.5 * magnitude**2 + 1.0
    return -0.5 * magnitude**3 + 2.5 * magnitude**2 - 4.0 * magnitude + 2.0


def apply_matrix(field, matrix, axis_dim):
    table = jnp.asarray(matrix, jnp.float32)
    if axis_dim == 2:
        return jnp.einsum("bil,lk->bik", field, table, precision=lax.Precision.HIGHEST)
    return jnp.einsum("bil,ik->bkl", field, table, precision=lax.Precision.HIGHEST)


def upsample_axis(extended, axis_dim):
    length = extended.shape[axis_dim]
    out_count = length - 4
    matrix = np.zeros((length, 4 * out_count), np.float32)
    positions = np.arange(out_count)
    for phase_index in range(4):
        position = (phase_index + 0.5) / 4.0 - 0.5
        floor_shift = math.floor(position)
        fraction = position - floor_shift
        for neighbour in (-1, 0, 1, 2):
            first_index = 2 + floor_shift + neighbour
            matrix[first_index + positions, 4 * positions + phase_index] += cubic_weight(
                fraction - neighbour
            )
    return apply_matrix(extended, matrix, axis_dim)


def upsample_tile(extended):
    return upsample_axis(upsample_axis(extended, 1), 2)


def analyze_axis(extended, tap_sets, offset, axis_dim):
    length = extended.shape[axis_dim]
    out_count = (length - 8) // 2
    positions = np.arange(out_count)
    results = []
    for tap_weights in tap_sets:
        matrix = np.zeros((length, out_count), np.float32)
        for tap_index in range(8):
            first_index = 4 - offset + tap_index
            matrix[first_index + 2 * positions, positions] += tap_weights[tap_index]
        results.append(apply_matrix(extended, matrix, axis_dim))
    return results


def synthesize_axis(low_ext, high_ext, lowpass, highpass, offset, axis_dim):
    present = [
        (member, tap_weights)
        for member, tap_weights in ((low_ext, lowpass), (high_ext, highpass))
        if member is not None
    ]
    length = present[0][0].shape[axis_dim]
    out_count = length - 4
    positions = np.arange(out_count)
    summed = None
    for member, tap_weights in present:
        matrix = np.zeros((length, 2 * out_count), np.float32)
        for parity in (0, 1):
            for tap_index in range(8):
                if (offset + parity - tap_index) % 2 == 0:
                    first_index = 2 + (offset + parity - tap_index) // 2
                    matrix[first_index + positions, 2 * positions + parity] += tap_weights[
                        tap_index
                    ]
        term = apply_matrix(member, matrix, axis_dim)
        summed = term if summed is None else summed + term
    return summed


def rows_full(col_low, col_high, row_tree):
    lowpass, highpass, offset = tree_filters(row_tree)
    low_low, low_high = analyze_axis(col_low, [lowpass, highpass], offset, 1)
    high_low, high_high = analyze_axis(col_high, [lowpass, highpass], offset, 1)
    return (low_low, (low_high, high_low, high_high))


def analyze_full(extended, col_tree, row_tree):
    lowpass, highpass, offset = tree_filters(col_tree)
    col_low, col_high = analyze_axis(extended, [lowpass, highpass], offset, 2)
    return rows_full(col_low, col_high, row_tree)


def analyze_low(extended, col_tree, row_tree):
    col_lowpass, col_highpass, col_offset = tree_filters(col_tree)
    row_lowpass, row_highpass, row_offset = tree_filters(row_tree)
    col_low = analyze_axis(extended, [col_lowpass], col_offset, 2)[0]
    return analyze_axis(col_low, [row_lowpass], row_offset, 1)[0]


def synthesize_tile(low_low, low_high, high_low, high_high, col_tree, row_tree):
    col_lowpass, col_highpass, col_offset = tree_filters(col_tree)
    row_lowpass, row_highpass, row_offset = tree_filters(row_tree)
    col_low = synthesize_axis(low_low, low_high, row_lowpass, row_highpass, row_offset, 1)
    col_high = synthesize_axis(high_low, high_high, row_lowpass, row_highpass, row_offset, 1)
    return synthesize_axis(col_low, col_high, col_lowpass, col_highpass, col_offset, 2)


def on_device(multispectral, panchromatic, band_gains):
    regrouped = lax.all_to_all(multispectral, "col", split_axis=2, concat_axis=0, tiled=True)
    pan_field = panchromatic[None]
    band_count = regrouped.shape[0]
    accumulated = None
    low_ext = extended_2(regrouped, (("row", 1), ("col", 2)), 2)
    upsampled = upsample_tile(low_ext)
    joined = extended_2(jnp.concatenate([upsampled, pan_field], 0), (("row", 1), ("col", 2)), 4)
    band_ext = joined[:band_count]
    pan_ext = joined[band_count:]
    for col_tree in range(2):
        col_lowpass, col_highpass, col_offset = tree_filters(col_tree)
        band_col = analyze_axis(band_ext, [col_lowpass], col_offset, 2)[0]
        pan_col_low, pan_col_high = analyze_axis(
            pan_ext, [col_lowpass, col_highpass], col_offset, 2
        )
        for row_tree in range(2):
            row_lowpass, row_highpass, row_offset = tree_filters(row_tree)
            band_low = analyze_axis(band_col, [row_lowpass], row_offset, 1)[0]
            pan_low, first_details = rows_full(pan_col_low, pan_col_high, row_tree)
            pan_details = [first_details]
            for level_index in range(1, LEVELS):
                joined_low = extended_2(
                    jnp.concatenate([band_low, pan_low], 0), (("row", 1), ("col", 2)), 4
                )
                band_low = analyze_low(joined_low[:band_count], col_tree, row_tree)
                pan_low, details = analyze_full(joined_low[band_count:], col_tree, row_tree)
                pan_details.append(details)
            current = band_low
            for level_index in reversed(range(LEVELS)):
                gains_now = band_gains[:, level_index][:, None, None]
                stacked = jnp.concatenate(
                    [current] + [gains_now * detail for detail in pan_details[level_index]], 0
                )
                extended = extended_2(stacked, (("row", 1), ("col", 2)), 2)
                current = synthesize_tile(
                    extended[:band_count],
                    extended[band_count : 2 * band_count],
                    extended[2 * band_count : 3 * band_count],
                    extended[3 * band_count :],
                    col_tree,
                    row_tree,
                )
            accumulated = current if accumulated is None else accumulated + current
    return 0.25 * accumulated


def solution(mesh):
    in_specs = (P("col", "row", None), P("row", "col"), P())
    out_specs = P(None, "row", "col")
    return jax.shard_map(
        on_device, mesh=mesh, in_specs=in_specs, out_specs=out_specs, check_vma=False
    )
```

profile of v0, /device:TPU:0, one launch (start us, length us, event | category | flops | bytes accessed | tf_op | source)
XLA Modules:
  0.0 526.4 jit_solution(549324112754145604)
XLA Ops:
  3.8 12.7 %all_to_all.18 = f32[8,1,4096]{2,1,0:T(1,128)S(1)} all-to-all(f32[8,1,4096]{2,1,0:T(1,128)S(1)} %reshape.314), channel_id=1, replica_groups=mesh['row'=16,'col'=8] {'col'}, dimensions={0} | all-to-all | bytes 262144 | tf_op jit(solution)/shard_map/all_to_all | solution.py:148
  18.8 5.3 %collective-permute-start.1 = (f32[8,2,128]{2,0,1:T(8,128)S(1)}, f32[8,2,128]{2,0,1:T(8,128)S(1)}, u32[]{:S(2)}, u32[]{:S(2)}) collective-permute-start(f32[8,2,128]{2,0,1:T(8,128)S(1)} %get-tuple-element.92), channel_id=1, source_target_pairs={{8,0},{16,8},{24,16},{32,24},{40,32},{48,40},{56,48},{64,56},{72,6... | collective-permute-start | bytes 24584 | tf_op jit(solution)/shard_map/ppermute | solution.py:33
  36.6 5.3 %collective-permute-start.5 = (f32[9,4,512]{2,1,0:T(4,128)S(1)}, f32[9,4,512]{2,1,0:T(4,128)S(1)}, u32[]{:S(2)}, u32[]{:S(2)}) collective-permute-start(f32[9,4,512]{2,1,0:T(4,128)S(1)} %get-tuple-element.16), channel_id=1, source_target_pairs={{8,0},{16,8},{24,16},{32,24},{40,32},{48,40},{56,48},{64,56},{72,6... | collective-permute-start | bytes 221192 | tf_op jit(solution)/shard_map/ppermute | solution.py:33
  50.3 6.2 %collective-permute-done.6 = f32[9,136,4]{1,2,0:T(4,128)S(1)} collective-permute-done((f32[9,136,4]{1,2,0:T(4,128)}, f32[9,136,4]{1,2,0:T(4,128)S(1)}, u32[]{:S(2)}, u32[]{:S(2)}) %collective-permute-start.6) | collective-permute-done | bytes 19616 | tf_op jit(solution)/shard_map/ppermute | solution.py:31
  75.1 5.3 %collective-permute-start.49 = (f32[9,4,256]{2,1,0:T(4,128)S(1)}, f32[9,4,256]{2,1,0:T(4,128)S(1)}, u32[]{:S(2)}, u32[]{:S(2)}) collective-permute-start(f32[9,4,256]{2,1,0:T(4,128)S(1)} %get-tuple-element.46), channel_id=1, source_target_pairs={{8,0},{16,8},{24,16},{32,24},{40,32},{48,40},{56,48},{64,56},{72,6... | collective-permute-start | bytes 110600 | tf_op jit(solution)/shard_map/ppermute | solution.py:33
  80.7 5.4 %collective-permute-start.29 = (f32[9,4,256]{2,1,0:T(4,128)S(1)}, f32[9,4,256]{2,1,0:T(4,128)S(1)}, u32[]{:S(2)}, u32[]{:S(2)}) collective-permute-start(f32[9,4,256]{2,1,0:T(4,128)S(1)} %get-tuple-element.44), channel_id=1, source_target_pairs={{8,0},{16,8},{24,16},{32,24},{40,32},{48,40},{56,48},{64,56},{72,6... | collective-permute-start | bytes 110600 | tf_op jit(solution)/shard_map/ppermute | solution.py:33
  88.4 5.3 %collective-permute-start.9 = (f32[9,4,256]{2,1,0:T(4,128)S(1)}, f32[9,4,256]{2,1,0:T(4,128)S(1)}, u32[]{:S(2)}, u32[]{:S(2)}) collective-permute-start(f32[9,4,256]{2,1,0:T(4,128)S(1)} %get-tuple-element.42), channel_id=1, source_target_pairs={{8,0},{16,8},{24,16},{32,24},{40,32},{48,40},{56,48},{64,56},{72,6... | collective-permute-start | bytes 110600 | tf_op jit(solution)/shard_map/ppermute | solution.py:33
  116.8 5.4 %collective-permute-done.70 = f32[9,72,4]{2,1,0:T(8,128)S(1)} collective-permute-done((f32[9,72,4]{2,1,0:T(8,128)S(1)}, f32[9,72,4]{2,1,0:T(8,128)S(1)}, u32[]{:S(2)}, u32[]{:S(2)}) %collective-permute-start.70) | collective-permute-done | bytes 10400 | tf_op jit(solution)/shard_map/ppermute | solution.py:31
  132.0 5.3 %collective-permute-start.33 = (f32[9,4,128]{2,1,0:T(4,128)S(1)}, f32[9,4,128]{2,1,0:T(4,128)S(1)}, u32[]{:S(2)}, u32[]{:S(2)}) collective-permute-start(f32[9,4,128]{2,1,0:T(4,128)S(1)} %get-tuple-element.86), channel_id=1, source_target_pairs={{8,0},{16,8},{24,16},{32,24},{40,32},{48,40},{56,48},{64,56},{72,6... | collective-permute-start | bytes 55304 | tf_op jit(solution)/shard_map/ppermute | solution.py:33
  138.8 5.3 %collective-permute-start.13 = (f32[9,4,128]{2,1,0:T(4,128)S(1)}, f32[9,4,128]{2,1,0:T(4,128)S(1)}, u32[]{:S(2)}, u32[]{:S(2)}) collective-permute-start(f32[9,4,128]{2,1,0:T(4,128)S(1)} %get-tuple-element.84), channel_id=1, source_target_pairs={{8,0},{16,8},{24,16},{32,24},{40,32},{48,40},{56,48},{64,56},{72,6... | collective-permute-start | bytes 55304 | tf_op jit(solution)/shard_map/ppermute | solution.py:33
  147.4 5.4 %collective-permute-start.73 = (f32[9,4,128]{2,1,0:T(4,128)S(1)}, f32[9,4,128]{2,1,0:T(4,128)S(1)}, u32[]{:S(2)}, u32[]{:S(2)}) collective-permute-start(f32[9,4,128]{2,1,0:T(4,128)S(1)} %get-tuple-element.90), channel_id=1, source_target_pairs={{8,0},{16,8},{24,16},{32,24},{40,32},{48,40},{56,48},{64,56},{72,6... | collective-permute-start | bytes 55304 | tf_op jit(solution)/shard_map/ppermute | solution.py:33
  153.0 5.4 %collective-permute-start.53 = (f32[9,4,128]{2,1,0:T(4,128)S(1)}, f32[9,4,128]{2,1,0:T(4,128)S(1)}, u32[]{:S(2)}, u32[]{:S(2)}) collective-permute-start(f32[9,4,128]{2,1,0:T(4,128)S(1)} %get-tuple-element.88), channel_id=1, source_target_pairs={{8,0},{16,8},{24,16},{32,24},{40,32},{48,40},{56,48},{64,56},{72,6... | collective-permute-start | bytes 55304 | tf_op jit(solution)/shard_map/ppermute | solution.py:33
  185.2 5.3 %collective-permute-start.17 = (f32[32,2,64]{2,1,0:T(2,128)S(1)}, f32[32,2,64]{2,1,0:T(2,128)S(1)}, u32[]{:S(2)}, u32[]{:S(2)}) collective-permute-start(f32[32,2,64]{2,1,0:T(2,128)S(1)} %get-tuple-element.66), channel_id=1, source_target_pairs={{8,0},{16,8},{24,16},{32,24},{40,32},{48,40},{56,48},{64,56},{72,6... | collective-permute-start | bytes 49160 | tf_op jit(solution)/shard_map/ppermute | solution.py:33
  190.6 5.3 %collective-permute-start.37 = (f32[32,2,64]{2,1,0:T(2,128)S(1)}, f32[32,2,64]{2,1,0:T(2,128)S(1)}, u32[]{:S(2)}, u32[]{:S(2)}) collective-permute-start(f32[32,2,64]{2,1,0:T(2,128)S(1)} %get-tuple-element.68), channel_id=1, source_target_pairs={{8,0},{16,8},{24,16},{32,24},{40,32},{48,40},{56,48},{64,56},{72,6... | collective-permute-start | bytes 49160 | tf_op jit(solution)/shard_map/ppermute | solution.py:33
  196.1 5.4 %collective-permute-start.57 = (f32[32,2,64]{2,1,0:T(2,128)S(1)}, f32[32,2,64]{2,1,0:T(2,128)S(1)}, u32[]{:S(2)}, u32[]{:S(2)}) collective-permute-start(f32[32,2,64]{2,1,0:T(2,128)S(1)} %get-tuple-element.70), channel_id=1, source_target_pairs={{8,0},{16,8},{24,16},{32,24},{40,32},{48,40},{56,48},{64,56},{72,6... | collective-permute-start | bytes 49160 | tf_op jit(solution)/shard_map/ppermute | solution.py:33
  201.8 5.4 %collective-permute-start.77 = (f32[32,2,64]{2,1,0:T(2,128)S(1)}, f32[32,2,64]{2,1,0:T(2,128)S(1)}, u32[]{:S(2)}, u32[]{:S(2)}) collective-permute-start(f32[32,2,64]{2,1,0:T(2,128)S(1)} %get-tuple-element.72), channel_id=1, source_target_pairs={{8,0},{16,8},{24,16},{32,24},{40,32},{48,40},{56,48},{64,56},{72,6... | collective-permute-start | bytes 49160 | tf_op jit(solution)/shard_map/ppermute | solution.py:33
  227.1 5.4 %collective-permute-done.58 = f32[32,20,2]{2,1,0:T(8,128)S(1)} collective-permute-done((f32[32,20,2]{2,1,0:T(8,128)S(1)}, f32[32,20,2]{2,1,0:T(8,128)S(1)}, u32[]{:S(2)}, u32[]{:S(2)}) %collective-permute-start.58) | collective-permute-done | bytes 5152 | tf_op jit(solution)/shard_map/ppermute | solution.py:31
  248.2 5.9 %collective-permute-start.21 = (f32[32,2,128]{2,1,0:T(2,128)S(1)}, f32[32,2,128]{2,1,0:T(2,128)S(1)}, u32[]{:S(2)}, u32[]{:S(2)}) collective-permute-start(f32[32,2,128]{2,1,0:T(2,128)S(1)} %get-tuple-element.50), channel_id=1, source_target_pairs={{8,0},{16,8},{24,16},{32,24},{40,32},{48,40},{56,48},{64,56},{72,6... | collective-permute-start | bytes 98312 | tf_op jit(solution)/shard_map/ppermute | solution.py:33
  255.0 5.4 %collective-permute-start.41 = (f32[32,2,128]{2,1,0:T(2,128)}, f32[32,2,128]{2,1,0:T(2,128)}, u32[]{:S(2)}, u32[]{:S(2)}) collective-permute-start(f32[32,2,128]{2,1,0:T(2,128)} %get-tuple-element.52), channel_id=1, source_target_pairs={{8,0},{16,8},{24,16},{32,24},{40,32},{48,40},{56,48},{64,56},{72,6... | collective-permute-start | bytes 98312 | tf_op jit(solution)/shard_map/ppermute | solution.py:33
  262.2 5.4 %collective-permute-start.61 = (f32[32,2,128]{2,1,0:T(2,128)}, f32[32,2,128]{2,1,0:T(2,128)}, u32[]{:S(2)}, u32[]{:S(2)}) collective-permute-start(f32[32,2,128]{2,1,0:T(2,128)} %get-tuple-element.54), channel_id=1, source_target_pairs={{8,0},{16,8},{24,16},{32,24},{40,32},{48,40},{56,48},{64,56},{72,6... | collective-permute-start | bytes 98312 | tf_op jit(solution)/shard_map/ppermute | solution.py:33
  357.6 5.4 %collective-permute-start.25 = (f32[32,2,256]{2,1,0:T(2,128)}, f32[32,2,256]{2,1,0:T(2,128)S(1)}, u32[]{:S(2)}, u32[]{:S(2)}) collective-permute-start(f32[32,2,256]{2,1,0:T(2,128)} %get-tuple-element.18), channel_id=1, source_target_pairs={{8,0},{16,8},{24,16},{32,24},{40,32},{48,40},{56,48},{64,56},{72,6... | collective-permute-start | bytes 196616 | tf_op jit(solution)/shard_map/ppermute | solution.py:33
  365.8 5.3 %collective-permute-start.85 = (f32[32,2,256]{2,1,0:T(2,128)S(1)}, f32[32,2,256]{2,1,0:T(2,128)S(1)}, u32[]{:S(2)}, u32[]{:S(2)}) collective-permute-start(f32[32,2,256]{2,1,0:T(2,128)S(1)} %get-tuple-element.24), channel_id=1, source_target_pairs={{8,0},{16,8},{24,16},{32,24},{40,32},{48,40},{56,48},{64,56},{72,6... | collective-permute-start | bytes 196616 | tf_op jit(solution)/shard_map/ppermute | solution.py:33
  373.1 5.4 %collective-permute-start.65 = (f32[32,2,256]{2,1,0:T(2,128)}, f32[32,2,256]{2,1,0:T(2,128)S(1)}, u32[]{:S(2)}, u32[]{:S(2)}) collective-permute-start(f32[32,2,256]{2,1,0:T(2,128)} %get-tuple-element.22), channel_id=1, source_target_pairs={{8,0},{16,8},{24,16},{32,24},{40,32},{48,40},{56,48},{64,56},{72,6... | collective-permute-start | bytes 196616 | tf_op jit(solution)/shard_map/ppermute | solution.py:33
  520.7 5.5 %add_multiply_fusion = f32[8,128,512]{2,1,0:T(8,128)} fusion(f32[8,128,512]{2,1,0:T(8,128)S(1)} %fusion.231, f32[8,128,512]{2,1,0:T(8,128)S(1)} %fusion.214, f32[8,128,512]{2,1,0:T(8,128)S(1)} %fusion.215, f32[8,128,512]{2,1,0:T(8,128)S(1)} %fusion.195, f32[8,128,512]{2,1,0:T(8,128)S(1)} %fusion.196, f32[8,128,512]{2,1,0:T(8,128)S(1)} %fusion.178, ...), kind=kOutput, calls=%fused_computation.9 | convolution fusion | flops 1639972864 | bytes 18374656 | tf_op jit(solution)/shard_map/bil,lk->bik/dot_general | solution.py:56
  (705 shorter events, 385.1 us)
Async XLA Ops:
  75.0 25.0 %collective-permute-start.48 = (f32[9,4,256]{2,1,0:T(4,128)S(1)}, f32[9,4,256]{2,1,0:T(4,128)S(1)}, u32[]{:S(2)}, u32[]{:S(2)}) collective-permute-start(f32[9,4,256]{2,1,0:T(4,128)S(1)} %get-tuple-element.45), channel_id=1, source_target_pairs={{0,8},{8,16},{16,24},{24,32},{32,40},{40,48},{48,56},{56,64},{64,7... | collective-permute-start | bytes 110600 | tf_op jit(solution)/shard_map/ppermute | solution.py:31
  75.1 29.1 %collective-permute-start.49 = (f32[9,4,256]{2,1,0:T(4,128)S(1)}, f32[9,4,256]{2,1,0:T(4,128)S(1)}, u32[]{:S(2)}, u32[]{:S(2)}) collective-permute-start(f32[9,4,256]{2,1,0:T(4,128)S(1)} %get-tuple-element.46), channel_id=1, source_target_pairs={{8,0},{16,8},{24,16},{32,24},{40,32},{48,40},{56,48},{64,56},{72,6... | collective-permute-start | bytes 110600 | tf_op jit(solution)/shard_map/ppermute | solution.py:33
  255.0 23.3 %collective-permute-start.41 = (f32[32,2,128]{2,1,0:T(2,128)}, f32[32,2,128]{2,1,0:T(2,128)}, u32[]{:S(2)}, u32[]{:S(2)}) collective-permute-start(f32[32,2,128]{2,1,0:T(2,128)} %get-tuple-element.52), channel_id=1, source_target_pairs={{8,0},{16,8},{24,16},{32,24},{40,32},{48,40},{56,48},{64,56},{72,6... | collective-permute-start | bytes 98312 | tf_op jit(solution)/shard_map/ppermute | solution.py:33
  261.3 26.9 %collective-permute-start.60 = (f32[32,2,128]{2,1,0:T(2,128)}, f32[32,2,128]{2,1,0:T(2,128)}, u32[]{:S(2)}, u32[]{:S(2)}) collective-permute-start(f32[32,2,128]{2,1,0:T(2,128)} %get-tuple-element.53), channel_id=1, source_target_pairs={{0,8},{8,16},{16,24},{24,32},{32,40},{40,48},{48,56},{56,64},{64,7... | collective-permute-start | bytes 98312 | tf_op jit(solution)/shard_map/ppermute | solution.py:31
  262.2 26.0 %collective-permute-start.61 = (f32[32,2,128]{2,1,0:T(2,128)}, f32[32,2,128]{2,1,0:T(2,128)}, u32[]{:S(2)}, u32[]{:S(2)}) collective-permute-start(f32[32,2,128]{2,1,0:T(2,128)} %get-tuple-element.54), channel_id=1, source_target_pairs={{8,0},{16,8},{24,16},{32,24},{40,32},{48,40},{56,48},{64,56},{72,6... | collective-permute-start | bytes 98312 | tf_op jit(solution)/shard_map/ppermute | solution.py:33
  267.6 31.3 %collective-permute-start.80 = (f32[32,2,128]{2,1,0:T(2,128)}, f32[32,2,128]{2,1,0:T(2,128)}, u32[]{:S(2)}, u32[]{:S(2)}) collective-permute-start(f32[32,2,128]{2,1,0:T(2,128)} %get-tuple-element.55), channel_id=1, source_target_pairs={{0,8},{8,16},{16,24},{24,32},{32,40},{40,48},{48,56},{56,64},{64,7... | collective-permute-start | bytes 98312 | tf_op jit(solution)/shard_map/ppermute | solution.py:31
  273.5 25.4 %collective-permute-start.81 = (f32[32,2,128]{2,1,0:T(2,128)}, f32[32,2,128]{2,1,0:T(2,128)}, u32[]{:S(2)}, u32[]{:S(2)}) collective-permute-start(f32[32,2,128]{2,1,0:T(2,128)} %get-tuple-element.56), channel_id=1, source_target_pairs={{8,0},{16,8},{24,16},{32,24},{40,32},{48,40},{56,48},{64,56},{72,6... | collective-permute-start | bytes 98312 | tf_op jit(solution)/shard_map/ppermute | solution.py:33
  278.3 33.1 %collective-permute-start.23 = (f32[32,36,2]{1,0,2:T(8,128)}, f32[32,36,2]{1,0,2:T(8,128)}, u32[]{:S(2)}, u32[]{:S(2)}) collective-permute-start(f32[32,36,2]{1,0,2:T(8,128)} %copy.211), channel_id=1, source_target_pairs={{1,0},{2,1},{3,2},{4,3},{5,4},{6,5},{7,6},{0,7},{9,8},{10,9},{11,1... | collective-permute-start | bytes 27656 | tf_op jit(solution)/shard_map/ppermute | solution.py:33
  288.2 21.2 %collective-permute-start.22 = (f32[32,36,2]{1,0,2:T(8,128)}, f32[32,36,2]{1,0,2:T(8,128)}, u32[]{:S(2)}, u32[]{:S(2)}) collective-permute-start(f32[32,36,2]{1,0,2:T(8,128)} %copy.210), channel_id=1, source_target_pairs={{0,1},{1,2},{2,3},{3,4},{4,5},{5,6},{6,7},{7,0},{8,9},{9,10},{10,1... | collective-permute-start | bytes 27656 | tf_op jit(solution)/shard_map/ppermute | solution.py:31
  288.2 36.7 %collective-permute-start.43 = (f32[32,36,2]{1,0,2:T(8,128)}, f32[32,36,2]{1,0,2:T(8,128)}, u32[]{:S(2)}, u32[]{:S(2)}) collective-permute-start(f32[32,36,2]{1,0,2:T(8,128)} %copy.219), channel_id=1, source_target_pairs={{1,0},{2,1},{3,2},{4,3},{5,4},{6,5},{7,6},{0,7},{9,8},{10,9},{11,1... | collective-permute-start | bytes 27656 | tf_op jit(solution)/shard_map/ppermute | solution.py:33
  298.9 23.7 %collective-permute-start.42 = (f32[32,36,2]{1,0,2:T(8,128)}, f32[32,36,2]{1,0,2:T(8,128)}, u32[]{:S(2)}, u32[]{:S(2)}) collective-permute-start(f32[32,36,2]{1,0,2:T(8,128)} %copy.218), channel_id=1, source_target_pairs={{0,1},{1,2},{2,3},{3,4},{4,5},{5,6},{6,7},{7,0},{8,9},{9,10},{10,1... | collective-permute-start | bytes 27656 | tf_op jit(solution)/shard_map/ppermute | solution.py:31
  298.9 34.9 %collective-permute-start.63 = (f32[32,36,2]{1,0,2:T(8,128)}, f32[32,36,2]{1,0,2:T(8,128)}, u32[]{:S(2)}, u32[]{:S(2)}) collective-permute-start(f32[32,36,2]{1,0,2:T(8,128)} %copy.227), channel_id=1, source_target_pairs={{1,0},{2,1},{3,2},{4,3},{5,4},{6,5},{7,6},{0,7},{9,8},{10,9},{11,1... | collective-permute-start | bytes 27656 | tf_op jit(solution)/shard_map/ppermute | solution.py:33
  309.4 22.5 %collective-permute-start.62 = (f32[32,36,2]{1,0,2:T(8,128)}, f32[32,36,2]{1,0,2:T(8,128)}, u32[]{:S(2)}, u32[]{:S(2)}) collective-permute-start(f32[32,36,2]{1,0,2:T(8,128)} %copy.226), channel_id=1, source_target_pairs={{0,1},{1,2},{2,3},{3,4},{4,5},{5,6},{6,7},{7,0},{8,9},{9,10},{10,1... | collective-permute-start | bytes 27656 | tf_op jit(solution)/shard_map/ppermute | solution.py:31
  311.4 31.3 %collective-permute-start.83 = (f32[32,36,2]{1,0,2:T(8,128)}, f32[32,36,2]{1,0,2:T(8,128)}, u32[]{:S(2)}, u32[]{:S(2)}) collective-permute-start(f32[32,36,2]{1,0,2:T(8,128)} %copy.235), channel_id=1, source_target_pairs={{1,0},{2,1},{3,2},{4,3},{5,4},{6,5},{7,6},{0,7},{9,8},{10,9},{11,1... | collective-permute-start | bytes 27656 | tf_op jit(solution)/shard_map/ppermute | solution.py:33
  357.6 50.5 %collective-permute-start.24 = (f32[32,2,256]{2,1,0:T(2,128)}, f32[32,2,256]{2,1,0:T(2,128)S(1)}, u32[]{:S(2)}, u32[]{:S(2)}) collective-permute-start(f32[32,2,256]{2,1,0:T(2,128)} %get-tuple-element.17), channel_id=1, source_target_pairs={{0,8},{8,16},{16,24},{24,32},{32,40},{40,48},{48,56},{56,64},{64,7... | collective-permute-start | bytes 196616 | tf_op jit(solution)/shard_map/ppermute | solution.py:31
  357.6 50.6 %collective-permute-start.25 = (f32[32,2,256]{2,1,0:T(2,128)}, f32[32,2,256]{2,1,0:T(2,128)S(1)}, u32[]{:S(2)}, u32[]{:S(2)}) collective-permute-start(f32[32,2,256]{2,1,0:T(2,128)} %get-tuple-element.18), channel_id=1, source_target_pairs={{8,0},{16,8},{24,16},{32,24},{40,32},{48,40},{56,48},{64,56},{72,6... | collective-permute-start | bytes 196616 | tf_op jit(solution)/shard_map/ppermute | solution.py:33
  364.3 33.5 %collective-permute-start.44 = (f32[32,2,256]{2,1,0:T(2,128)}, f32[32,2,256]{2,1,0:T(2,128)S(1)}, u32[]{:S(2)}, u32[]{:S(2)}) collective-permute-start(f32[32,2,256]{2,1,0:T(2,128)} %get-tuple-element.19), channel_id=1, source_target_pairs={{0,8},{8,16},{16,24},{24,32},{32,40},{40,48},{48,56},{56,64},{64,7... | collective-permute-start | bytes 196616 | tf_op jit(solution)/shard_map/ppermute | solution.py:31
  385.5 31.3 %collective-permute-start.87 = (f32[32,68,2]{1,0,2:T(8,128)}, f32[32,68,2]{1,0,2:T(8,128)}, u32[]{:S(2)}, u32[]{:S(2)}) collective-permute-start(f32[32,68,2]{1,0,2:T(8,128)} %copy.239), channel_id=1, source_target_pairs={{1,0},{2,1},{3,2},{4,3},{5,4},{6,5},{7,6},{0,7},{9,8},{10,9},{11,1... | collective-permute-start | bytes 52232 | tf_op jit(solution)/shard_map/ppermute | solution.py:33
  397.9 38.4 %collective-permute-start.67 = (f32[32,68,2]{1,0,2:T(8,128)}, f32[32,68,2]{1,0,2:T(8,128)}, u32[]{:S(2)}, u32[]{:S(2)}) collective-permute-start(f32[32,68,2]{1,0,2:T(8,128)} %copy.231), channel_id=1, source_target_pairs={{1,0},{2,1},{3,2},{4,3},{5,4},{6,5},{7,6},{0,7},{9,8},{10,9},{11,1... | collective-permute-start | bytes 52232 | tf_op jit(solution)/shard_map/ppermute | solution.py:33
  408.2 25.4 %collective-permute-start.66 = (f32[32,68,2]{1,0,2:T(8,128)}, f32[32,68,2]{1,0,2:T(8,128)}, u32[]{:S(2)}, u32[]{:S(2)}) collective-permute-start(f32[32,68,2]{1,0,2:T(8,128)} %copy.230), channel_id=1, source_target_pairs={{0,1},{1,2},{2,3},{3,4},{4,5},{5,6},{6,7},{7,0},{8,9},{9,10},{10,1... | collective-permute-start | bytes 52232 | tf_op jit(solution)/shard_map/ppermute | solution.py:31
  408.2 43.1 %collective-permute-start.47 = (f32[32,68,2]{1,0,2:T(8,128)}, f32[32,68,2]{1,0,2:T(8,128)}, u32[]{:S(2)}, u32[]{:S(2)}) collective-permute-start(f32[32,68,2]{1,0,2:T(8,128)} %copy.223), channel_id=1, source_target_pairs={{1,0},{2,1},{3,2},{4,3},{5,4},{6,5},{7,6},{0,7},{9,8},{10,9},{11,1... | collective-permute-start | bytes 52232 | tf_op jit(solution)/shard_map/ppermute | solution.py:33
  415.3 33.6 %collective-permute-start.46 = (f32[32,68,2]{1,0,2:T(8,128)}, f32[32,68,2]{1,0,2:T(8,128)}, u32[]{:S(2)}, u32[]{:S(2)}) collective-permute-start(f32[32,68,2]{1,0,2:T(8,128)} %copy.222), channel_id=1, source_target_pairs={{0,1},{1,2},{2,3},{3,4},{4,5},{5,6},{6,7},{7,0},{8,9},{9,10},{10,1... | collective-permute-start | bytes 52232 | tf_op jit(solution)/shard_map/ppermute | solution.py:31
  416.8 49.5 %collective-permute-start.27 = (f32[32,68,2]{1,0,2:T(8,128)}, f32[32,68,2]{1,0,2:T(8,128)}, u32[]{:S(2)}, u32[]{:S(2)}) collective-permute-start(f32[32,68,2]{1,0,2:T(8,128)} %copy.215), channel_id=1, source_target_pairs={{1,0},{2,1},{3,2},{4,3},{5,4},{6,5},{7,6},{0,7},{9,8},{10,9},{11,1... | collective-permute-start | bytes 52232 | tf_op jit(solution)/shard_map/ppermute | solution.py:33
  433.6 30.3 %collective-permute-start.26 = (f32[32,68,2]{1,0,2:T(8,128)}, f32[32,68,2]{1,0,2:T(8,128)}, u32[]{:S(2)}, u32[]{:S(2)}) collective-permute-start(f32[32,68,2]{1,0,2:T(8,128)} %copy.214), channel_id=1, source_target_pairs={{0,1},{1,2},{2,3},{3,4},{4,5},{5,6},{6,7},{7,0},{8,9},{9,10},{10,1... | collective-permute-start | bytes 52232 | tf_op jit(solution)/shard_map/ppermute | solution.py:31
  (193 other events, 4578.2 us)
where the time goes:
time: 536 us; the launch traced here: 526 us
  starting transfers between devices  192 us (36%)
  matrix products  136 us (25%)
  local copies, waits for them, and re-layouts  83.2 us (16%)
  waiting for transfers between devices  53 us (10%)
  other arithmetic  45.5 us (8%)
  blocking collectives  12.7 us (2%)
    ppermute x44, starting transfers between devices, extended_2(): lax.ppermute(head, axis, [((i + 1) % count, i) for i in range(count)])  188 us
    dot_general x105, matrix products, apply_matrix(): jnp.einsum('bil,ik->bkl', field, table, precision=lax.Precision.HIGHEST)  78.5 us
    dot_general x55, matrix products, apply_matrix(): jnp.einsum('bil,lk->bik', field, table, precision=lax.Precision.HIGHEST)  57.7 us
    ppermute x44, waiting for transfers between devices, extended_2(): lax.ppermute(tail, axis, [(i, (i + 1) % count) for i in range(count)])  52.2 us
    concatenate x33, other arithmetic, extended_2(): jnp.concatenate([lax.ppermute(tail, axis, [(i, (i + 1) % count) for i in...  33.3 us
    slice x31, local copies, waits for them, and re-layouts, extended_2(): lax.slice_in_dim(cells, cells.shape[dim] - width, cells.shape[dim], axis=...  29.1 us
    ppermute x9, local copies, waits for them, and re-layouts, extended_2(): lax.ppermute(head, axis, [((i + 1) % count, i) for i in range(count)])  17 us
    ppermute x9, local copies, waits for them, and re-layouts, extended_2(): lax.ppermute(tail, axis, [(i, (i + 1) % count) for i in range(count)])  16.5 us
  transfers between devices with their start and end apart: 88, of which 18 were waited for; matrix products, arithmetic and copies ran while one was open for 28% of the time, Pallas kernels for 0%

commit v1 on v0

v1 whole, which is shorter than its diff:
```python
import functools
import math

import jax
import jax.numpy as jnp
import ml_dtypes
import numpy as np
from jax import lax
from jax.experimental import pallas as pl
from jax.experimental.pallas import tpu as pltpu
from jax.sharding import PartitionSpec as P

MESH = pl.DeviceIdType.MESH
BF16 = ml_dtypes.bfloat16

TAPS = [
    0.2303778133088964,
    0.7148465705529154,
    0.6308807679298587,
    -0.0279837694168599,
    -0.1870348117190931,
    0.0308413818355607,
    0.0328830116668852,
    -0.0105974017850690,
]

ROWS, COLS = 128, 512
LROWS, LCOLS = 32, 128
PAN_RIM = 48
PAN_EXT = ROWS + 2 * PAN_RIM
MS_RIM = 16
BANDS = 8


def projection(level):
    step = 2**level
    rows = [{} for _ in range(8)]
    for tree in range(2):
        taps = TAPS if tree == 0 else TAPS[::-1]
        cascade, shift = [1.0], 0
        for lev in range(level):
            longer = [0.0] * (len(cascade) + 7 * 2**lev)
            for i, value in enumerate(cascade):
                for j, tap in enumerate(taps):
                    longer[i + j * 2**lev] += value * tap
            cascade, shift = longer, shift + (3 + tree) * 2**lev
        span = len(cascade)
        for m in range(8):
            for k in range(-64, 64):
                at = m - step * k + shift
                if 0 <= at < span:
                    for i, value in enumerate(cascade):
                        offset = step * k - shift + i - m
                        rows[m][offset] = rows[m].get(offset, 0.0) + 0.5 * cascade[at] * value
    return rows


def cubic_weight(distance):
    magnitude = abs(distance)
    if magnitude <= 1.0:
        return 1.5 * magnitude**3 - 2.5 * magnitude**2 + 1.0
    if magnitude < 2.0:
        return -0.5 * magnitude**3 + 2.5 * magnitude**2 - 4.0 * magnitude + 2.0
    return 0.0


def upsampled_projection():
    rows = [{} for _ in range(8)]
    for m, weights in enumerate(projection(3)):
        for offset in sorted(weights):
            position = (m + offset + 0.5) / 4.0 - 0.5
            floor = math.floor(position)
            for low in range(floor - 1, floor + 3):
                term = weights[offset] * cubic_weight(position - low)
                rows[m][low] = rows[m].get(low, 0.0) + term
    return rows


def split_parts(matrix):
    high = matrix.astype(np.float32).astype(BF16)
    low = (matrix - high.astype(np.float64)).astype(np.float32).astype(BF16)
    return high, low


def pan_matrix(level, outs, ins, start):
    matrix = np.zeros((outs, ins))
    rows = projection(level)
    for m in range(outs):
        for offset, weight in rows[m % 8].items():
            matrix[m, m + offset - start] = weight
    return matrix


def ms_matrix(outs, lows):
    place = {low: at for at, low in lows}
    matrix = np.zeros((outs, max(at for at, _ in lows) + 1))
    rows = upsampled_projection()
    for m in range(outs):
        for low, weight in rows[m % 8].items():
            matrix[m, place[low + 2 * (m // 8)]] = weight
    return matrix


def make_tables():
    high, low = split_parts(ms_matrix(ROWS, [(i, i - MS_RIM) for i in range(LROWS + 2 * MS_RIM)]))
    ms_rows = np.concatenate([high, high, low], 1)
    lows = [(i, i) for i in range(LCOLS)]
    lows += [(LCOLS + i, i - MS_RIM) for i in range(MS_RIM)]
    lows += [(LCOLS + MS_RIM + i, LCOLS + i) for i in range(MS_RIM)]
    matrix = ms_matrix(COLS, lows)
    matrix = np.pad(matrix, ((0, 0), (0, 256 - matrix.shape[1]))).T
    high, low = split_parts(matrix)
    ms_cols = np.concatenate([high, high, low], 0)
    matrix = np.concatenate([pan_matrix(level, 128, 256, -64) for level in (1, 2, 3)], 0).T
    high, low = split_parts(matrix)
    pan_cols = np.concatenate([high, high, low], 0)
    pan_rows = []
    for level in (1, 2, 3):
        high, low = split_parts(pan_matrix(level, ROWS, PAN_EXT, -PAN_RIM))
        pan_rows.append(np.concatenate([high, high, low], 1))
    return ms_rows, ms_cols, pan_cols, np.stack(pan_rows)


def parts_of(x):
    high = x.astype(jnp.bfloat16)
    low = (x - high.astype(jnp.float32)).astype(jnp.bfloat16)
    return high, low


def kernel(
    nr, nc,
    ms_hbm, pan_hbm, gains, ms_rows_hbm, ms_cols_hbm, pan_cols_hbm, pan_rows_hbm,
    out_ref,
    ms_own, stage, mbuf, pan_ext, pstage, precv,
    ms_rows, ms_cols, pan_cols, pan_rows,
    pan_split, zbuf, qbuf, xsplit, ybuf,
    load_sems, own_sem, ms_send, ms_recv, pan_send, pan_recv,
):
    r, c = lax.axis_index("row"), lax.axis_index("col")
    row_of = {d: lax.rem(r + d + nr, nr) for d in (-1, 0, 1)}
    col_of = [lax.rem(c + k, nc) for k in range(nc)]

    barrier = pltpu.get_barrier_semaphore()
    for d in (-1, 0, 1):
        for k in range(nc):
            if d or k:
                pl.semaphore_signal(
                    barrier, inc=1, device_id=(row_of[d], col_of[k]), device_id_type=MESH
                )

    ms_load = pltpu.make_async_copy(ms_hbm.at[0], ms_own, load_sems.at[0])
    pan_load = pltpu.make_async_copy(
        pan_hbm, pan_ext.at[PAN_RIM : PAN_RIM + ROWS], load_sems.at[1]
    )
    table_loads = [
        pltpu.make_async_copy(source, target, load_sems.at[2 + i])
        for i, (source, target) in enumerate(
            (
                (pan_cols_hbm, pan_cols),
                (pan_rows_hbm, pan_rows),
                (ms_cols_hbm, ms_cols),
                (ms_rows_hbm, ms_rows),
            )
        )
    ]
    ms_load.start()
    pan_load.start()
    for load in table_loads:
        load.start()

    lane = lax.broadcasted_iota(jnp.int32, (8, 128), 1)

    ms_load.wait()
    for dest in range(nc):
        tile = slice(128 * dest, 128 * dest + 128)
        before = (dest - 1) % nc
        after = (dest + 1) % nc
        stage[dest, 0:16] = ms_own[0:16, tile]
        stage[dest, 24:40] = ms_own[16:32, tile]
        rim = None
        for q in range(4):
            rows = slice(8 * q, 8 * q + 8)
            both = jnp.where(
                lane < 64,
                ms_own[rows, 128 * after : 128 * after + 128],
                ms_own[rows, 128 * before : 128 * before + 128],
            )
            both = pltpu.roll(both, (16 + 32 * q) % 128, 1)
            rim = both if rim is None else jnp.where(lane < 32 * q, rim, both)
        stage[dest, 16:24] = rim

    pan_load.wait()
    for at, (first, count) in ((0, (0, 64)), (64, (80, 24)), (88, (0, 24))):
        for step in range(0, count, 8):
            upper = PAN_RIM + first + step
            lower = upper + count
            for side, column in ((0, 384), (1, 0)):
                one = pan_ext[upper : upper + 8, column : column + 128]
                two = pan_ext[lower : lower + 8, column : column + 128]
                if side == 0:
                    packed = jnp.where(lane < 64, pltpu.roll(one, 64, 1), two)
                else:
                    packed = jnp.where(lane < 64, one, pltpu.roll(two, 64, 1))
                pstage[side, at + step : at + step + 8] = packed

    pl.semaphore_wait(barrier, 3 * nc - 1)

    def remote(source, target, send_sem, recv_sem, d, k):
        return pltpu.make_async_remote_copy(
            src_ref=source,
            dst_ref=target,
            send_sem=send_sem,
            recv_sem=recv_sem,
            device_id=(row_of[d], col_of[k % nc]),
            device_id_type=MESH,
        )

    pan_copies = []
    own = PAN_RIM
    for d, source, target in (
        (1, pan_ext.at[own + ROWS - PAN_RIM : own + ROWS], pan_ext.at[0:PAN_RIM]),
        (-1, pan_ext.at[own : own + PAN_RIM], pan_ext.at[own + ROWS : PAN_EXT]),
    ):
        at = len(pan_copies)
        pan_copies.append(remote(source, target, pan_send.at[at], pan_recv.at[at], d, 0))
    for side, k in ((0, 1), (1, -1)):
        for d, rows in ((0, slice(0, 64)), (1, slice(64, 88)), (-1, slice(88, 112))):
            at = len(pan_copies)
            pan_copies.append(
                remote(
                    pstage.at[side, rows], precv.at[side, rows],
                    pan_send.at[at], pan_recv.at[at], d, k,
                )
            )
    ms_copies = []
    spans = {0: (slice(0, 40), slice(24, 64)), 1: (slice(16, 40), slice(0, 24)), -1: (slice(0, 24), slice(64, 88))}
    for d in (0, 1, -1):
        source, target = spans[d]
        for k in range(nc):
            if d or k:
                ms_copies.append(
                    remote(
                        stage.at[col_of[k], source], mbuf.at[c, target],
                        ms_send.at[d + 1, k], ms_recv.at[d + 1, c], d, k,
                    )
                )
    own_copy = pltpu.make_async_copy(stage.at[c], mbuf.at[c, 24:64], own_sem)
    for copy in pan_copies + ms_copies:
        copy.start()
    own_copy.start()

    for copy in pan_copies:
        copy.wait_recv()
    for step in range(0, PAN_EXT, 8):
        rows = slice(step, step + 8)
        if step < 48:
            base, at, half = 0, 64, 24
        elif step < 176:
            base, at, half = 48, 0, 64
        else:
            base, at, half = 176, 88, 24
        second = step - base >= half
        inside = step - base - (half if second else 0)
        left = precv[0, at + inside : at + inside + 8]
        right = precv[1, at + inside : at + inside + 8]
        if second:
            left = pltpu.roll(left, 64, 1)
        else:
            right = pltpu.roll(right, 64, 1)
        tiles = [left]
        tiles += [pltpu.roll(pan_ext[rows, 128 * t : 128 * t + 128], 64, 1) for t in range(4)]
        tiles += [right]
        for t in range(5):
            value = jnp.where(lane < 64, tiles[t], tiles[t + 1])
            high, low = parts_of(value)
            pan_split[0, rows, 128 * t : 128 * t + 128] = high.astype(jnp.float32)
            pan_split[1, rows, 128 * t : 128 * t + 128] = low.astype(jnp.float32)

    for load in table_loads:
        load.wait()
    for j in range(4):
        window = slice(128 * j, 128 * j + 256)
        high = pan_split[0, :, window].astype(jnp.bfloat16)
        low = pan_split[1, :, window].astype(jnp.bfloat16)
        z = jnp.dot(
            jnp.concatenate([high, low, high], 1), pan_cols[...], preferred_element_type=jnp.float32
        )
        for level in range(3):
            high, low = parts_of(z[:, 128 * level : 128 * level + 128])
            for at, part in ((0, high), (1, low), (2, high)):
                zbuf[level, PAN_EXT * at : PAN_EXT * (at + 1), 128 * j : 128 * j + 128] = part
    for level in range(3):
        qbuf[level] = jnp.dot(pan_rows[level], zbuf[level], preferred_element_type=jnp.float32)

    own_copy.wait()
    for d in (-1, 0, 1):
        source, target = spans[d]
        for k in range(nc):
            if d or k:
                remote(
                    stage.at[col_of[k], source], mbuf.at[col_of[k], target],
                    ms_send.at[d + 1, k], ms_recv.at[1 - d if d else 1, col_of[k]], d, k,
                ).wait_recv()

    def gather_band(b, carry):
        for g, (main, rim, q) in enumerate(
            (
                (8, 0, 2), (16, 0, 3),
                (24, 40, 0), (32, 40, 1), (48, 40, 2), (56, 40, 3),
                (64, 80, 0), (72, 80, 1),
            )
        ):
            rows = pl.ds(pl.multiple_of(64 * b, 64) + 8 * g, 8)
            edge = mbuf[b, rim : rim + 8]
            if q:
                edge = pltpu.roll(edge, 128 - 32 * q, 1)
            xsplit[rows, 0:128] = mbuf[b, main : main + 8]
            xsplit[rows, 128:256] = edge
        return carry

    lax.fori_loop(0, BANDS, gather_band, 0)
    high, low = parts_of(xsplit[...])
    ybuf[...] = jnp.dot(
        jnp.concatenate([high, low, high], 1), ms_cols[...], preferred_element_type=jnp.float32
    )

    def finish_band(b, carry):
        g1, g2, g3 = gains[0, b], gains[1, b], gains[2, b]
        high, low = parts_of(ybuf[pl.ds(pl.multiple_of(64 * b, 64), 64)])
        total = jnp.dot(
            ms_rows[...], jnp.concatenate([high, low, high], 0), preferred_element_type=jnp.float32
        )
        total += g1 * pan_ext[PAN_RIM : PAN_RIM + ROWS]
        total += (g2 - g1) * qbuf[0] + (g3 - g2) * qbuf[1] - g3 * qbuf[2]
        out_ref[b] = total
        return carry

    lax.fori_loop(0, BANDS, finish_band, 0)

    for copy in pan_copies + ms_copies:
        copy.wait_send()


def on_device(nr, nc, tables, ms, pan, gains):
    f32 = jnp.float32
    bf16 = jnp.bfloat16
    hbm = pl.BlockSpec(memory_space=pl.ANY)
    return pl.pallas_call(
        functools.partial(kernel, nr, nc),
        out_shape=jax.ShapeDtypeStruct((BANDS, ROWS, COLS), f32),
        in_specs=[hbm, hbm, pl.BlockSpec(memory_space=pltpu.SMEM)] + [hbm] * 4,
        out_specs=pl.BlockSpec(memory_space=pltpu.VMEM),
        scratch_shapes=[
            pltpu.VMEM((LROWS, nc * LCOLS), f32),
            pltpu.VMEM((nc, 40, 128), f32),
            pltpu.VMEM((BANDS, 88, 128), f32),
            pltpu.VMEM((PAN_EXT, COLS), f32),
            pltpu.VMEM((2, 112, 128), f32),
            pltpu.VMEM((2, 112, 128), f32),
            *[pltpu.VMEM(table.shape, bf16) for table in tables],
            pltpu.VMEM((2, PAN_EXT, COLS + 128), f32),
            pltpu.VMEM((3, 3 * PAN_EXT, COLS), bf16),
            pltpu.VMEM((3, ROWS, COLS), f32),
            pltpu.VMEM((BANDS * 64, 256), f32),
            pltpu.VMEM((BANDS * 64, COLS), f32),
            pltpu.SemaphoreType.DMA((6,)),
            pltpu.SemaphoreType.DMA,
            pltpu.SemaphoreType.DMA((3, nc)),
            pltpu.SemaphoreType.DMA((3, nc)),
            pltpu.SemaphoreType.DMA((8,)),
            pltpu.SemaphoreType.DMA((8,)),
        ],
        compiler_params=pltpu.CompilerParams(
            collective_id=0, has_side_effects=True, vmem_limit_bytes=32 * 1024 * 1024
        ),
    )(ms, pan, gains.T, *[jnp.asarray(table) for table in tables])


def solution(mesh):
    tables = make_tables()
    nr, nc = mesh.shape["row"], mesh.shape["col"]
    return jax.shard_map(
        functools.partial(on_device, nr, nc, tables),
        mesh=mesh,
        in_specs=(P("col", "row", None), P("row", "col"), P()),
        out_specs=P(None, "row", "col"),
        check_vma=False,
    )
```

time: 536 us -> 29.1 us (0.05); the launches traced: 526 us -> 28.7 us
  starting transfers between devices: 192 us -> 0 us
  matrix products: 136 us -> 0 us
  local copies, waits for them, and re-layouts: 83.2 us -> 7.95 us
  waiting for transfers between devices: 53 us -> 0 us
  other arithmetic: 45.5 us -> 0 us
  Pallas kernels: 0 us -> 20.8 us
  blocking collectives: 12.7 us -> 0 us
    ppermute x88 -> x0, starting transfers between devices: 192 us -> none  [the longest x44 188 us: extended_2(): lax.ppermute(head, axis, [((i + 1) % count, i) for i in range(count)])]
    dot_general x160 -> x0, matrix products: 136 us -> none  [the longest x105 78.5 us: apply_matrix(): jnp.einsum('bil,ik->bkl', field, table, precision=lax.Precision.HIGHEST)]
    ppermute x88 -> x0, waiting for transfers between devices: 53 us -> none  [the longest x44 52.2 us: extended_2(): lax.ppermute(tail, axis, [(i, (i + 1) % count) for i in range(count)])]
    slice x40 -> x0, local copies, waits for them, and re-layouts: 44.2 us -> none  [the longest x31 29.1 us: extended_2(): lax.slice_in_dim(cells, cells.shape[dim] - width, cells.shape[dim], axis=...]
    ppermute x18 -> x0, local copies, waits for them, and re-layouts: 33.5 us -> none  [the longest x9 17 us: extended_2(): lax.ppermute(head, axis, [((i + 1) % count, i) for i in range(count)])]
    concatenate x33 -> x0, other arithmetic: 33.3 us -> none  [extended_2(): jnp.concatenate([lax.ppermute(tail, axis, [(i, (i + 1) % count) for i in...]
    pallas_call x0 -> x1, Pallas kernels: none -> 20.8 us  [on_device(): pl.pallas_call(functools.partial(kernel, nr, nc), out_shape=jax.ShapeDtyp...]
    all_to_all x1 -> x0, blocking collectives: 12.7 us -> none  [on_device(): lax.all_to_all(multispectral, 'col', split_axis=2, concat_axis=0, tiled=T...]
  transfers between devices with their start and end apart: 88 -> 0, of which waited for: 18 -> 0; matrix products, arithmetic and copies ran while one was open for 28% -> 0% of each run, Pallas kernels for 0% -> 0%
where the time goes in v1:
time: 29.1 us; the launch traced here: 28.7 us
  Pallas kernels  20.8 us (71%)
  local copies, waits for them, and re-layouts  7.95 us (27%)
    pallas_call x1, Pallas kernels, on_device(): pl.pallas_call(functools.partial(kernel, nr, nc), out_shape=jax.ShapeDtyp...  20.8 us
    unnamed x15, local copies, waits for them, and re-layouts  7.95 us

profile of v1, /device:TPU:0, one launch (start us, length us, event | category | flops | bytes accessed | tf_op | source)
XLA Modules:
  0.0 28.7 jit_solution(5805430638942945759)
XLA Ops:
  0.0 0.0 copy-start
  0.0 1.1 %copy-done = bf16[768,512]{1,0:T(8,128)(2,1)S(1)} copy-done((bf16[768,512]{1,0:T(8,128)(2,1)S(1)}, bf16[768,512]{1,0:T(8,128)(2,1)}, u32[]{:S(2)}) %copy-start) | copy-done | bytes 786456
  1.1 0.0 copy-start.1
  1.1 1.1 %copy-done.1 = bf16[3,128,672]{2,1,0:T(8,128)(2,1)S(1)} copy-done((bf16[3,128,672]{2,1,0:T(8,128)(2,1)S(1)}, bf16[3,128,672]{2,1,0:T(8,128)(2,1)}, u32[]{:S(2)}) %copy-start.1) | copy-done | bytes 516120
  2.2 0.0 copy-start.2
  2.2 1.1 %copy-done.2 = bf16[768,384]{1,0:T(8,128)(2,1)S(1)} copy-done((bf16[768,384]{1,0:T(8,128)(2,1)S(1)}, bf16[768,384]{1,0:T(8,128)(2,1)}, u32[]{:S(2)}) %copy-start.2) | copy-done | bytes 589848
  3.3 0.0 copy-start.3
  3.3 0.9 %copy-done.3 = f32[128,512]{1,0:T(8,128)S(1)} copy-done((f32[128,512]{1,0:T(8,128)S(1)}, f32[128,512]{1,0:T(8,128)}, u32[]{:S(2)}) %copy-start.3) | copy-done | bytes 262168
  4.2 0.0 copy-start.4
  4.2 0.9 %copy-done.4 = f32[1,32,1024]{2,1,0:T(8,128)S(1)} copy-done((f32[1,32,1024]{2,1,0:T(8,128)S(1)}, f32[1,32,1024]{2,1,0:T(8,128)}, u32[]{:S(2)}) %copy-start.4) | copy-done | bytes 131096
  5.1 0.0 copy-start.5
  5.1 0.8 %copy-done.5 = bf16[128,192]{1,0:T(8,128)(2,1)S(1)} copy-done((bf16[128,192]{1,0:T(8,128)(2,1)S(1)}, bf16[128,192]{1,0:T(8,128)(2,1)}, u32[]{:S(2)}) %copy-start.5) | copy-done | bytes 49176
  6.0 0.0 copy-start.6
  6.0 0.7 %copy-done.6 = f32[8,3]{0,1:T(4,128)S(1)} copy-done((f32[8,3]{0,1:T(4,128)S(1)}, f32[8,3]{0,1:T(4,128)}, u32[]{:S(2)}) %copy-start.6) | copy-done | bytes 120
  6.6 20.8 %shard_map.73 = f32[8,128,512]{2,1,0:T(8,128)S(1)} custom-call(f32[1,32,1024]{2,1,0:T(8,128)S(1)} %copy-done.4, f32[128,512]{1,0:T(8,128)S(1)} %copy-done.3, f32[3,8]{1,0:T(4,128)S(1)} %bitcast.1, bf16[128,192]{1,0:T(8,128)(2,1)S(1)} %copy-done.5, bf16[768,512]{1,0:T(8,128)(2,1)S(1)} %copy-done, bf16[768,384]{1,0:T(8,128)(2,1)S(1)} %copy-done.2, ...), custom_call_target="tpu_custom_call" | custom-call | tf_op jit(solution)/shard_map/pallas_call | solution.py:348
  27.4 1.3 %copy.9 = f32[8,128,512]{2,1,0:T(8,128)} copy(f32[8,128,512]{2,1,0:T(8,128)S(1)} %shard_map.73) | data formatting | bytes 4194304
Async XLA Ops:
  0.0 1.1 %copy-start = (bf16[768,512]{1,0:T(8,128)(2,1)S(1)}, bf16[768,512]{1,0:T(8,128)(2,1)}, u32[]{:S(2)}) copy-start(bf16[768,512]{1,0:T(8,128)(2,1)} %constant.9.clone.ms_cols_hbm) | copy-start | bytes 2359300
  1.1 1.1 %copy-start.1 = (bf16[3,128,672]{2,1,0:T(8,128)(2,1)S(1)}, bf16[3,128,672]{2,1,0:T(8,128)(2,1)}, u32[]{:S(2)}) copy-start(bf16[3,128,672]{2,1,0:T(8,128)(2,1)} %constant.11.clone.pan_rows_hbm) | copy-start | bytes 1548292
  2.2 1.1 %copy-start.2 = (bf16[768,384]{1,0:T(8,128)(2,1)S(1)}, bf16[768,384]{1,0:T(8,128)(2,1)}, u32[]{:S(2)}) copy-start(bf16[768,384]{1,0:T(8,128)(2,1)} %constant.10.clone.pan_cols_hbm) | copy-start | bytes 1769476
  3.3 0.9 %copy-start.3 = (f32[128,512]{1,0:T(8,128)S(1)}, f32[128,512]{1,0:T(8,128)}, u32[]{:S(2)}) copy-start(f32[128,512]{1,0:T(8,128)} %pan_hbm.1) | copy-start | bytes 786436
  4.2 0.9 %copy-start.4 = (f32[1,32,1024]{2,1,0:T(8,128)S(1)}, f32[1,32,1024]{2,1,0:T(8,128)}, u32[]{:S(2)}) copy-start(f32[1,32,1024]{2,1,0:T(8,128)} %ms_hbm.1) | copy-start | bytes 393220
  5.1 0.8 %copy-start.5 = (bf16[128,192]{1,0:T(8,128)(2,1)S(1)}, bf16[128,192]{1,0:T(8,128)(2,1)}, u32[]{:S(2)}) copy-start(bf16[128,192]{1,0:T(8,128)(2,1)} %constant.8.clone.ms_rows_hbm) | copy-start | bytes 147460
  6.0 0.7 %copy-start.6 = (f32[8,3]{0,1:T(4,128)S(1)}, f32[8,3]{0,1:T(4,128)}, u32[]{:S(2)}) copy-start(f32[8,3]{0,1:T(4,128)} %param.9) | copy-start | bytes 292

commit v2 on v1

--- a/solution.py
+++ b/solution.py
@@ -129,12 +129,12 @@
 
 def kernel(
     nr, nc,
-    ms_hbm, pan_hbm, gains, ms_rows_hbm, ms_cols_hbm, pan_cols_hbm, pan_rows_hbm,
+    ms_hbm, pan_hbm, gains_hbm, ms_rows_hbm, ms_cols_hbm, pan_cols_hbm, pan_rows_hbm,
     out_ref,
     ms_own, stage, mbuf, pan_ext, pstage, precv,
     ms_rows, ms_cols, pan_cols, pan_rows,
     pan_split, zbuf, qbuf, xsplit, ybuf,
-    load_sems, own_sem, ms_send, ms_recv, pan_send, pan_recv,
+    gains, load_sems, own_sem, ms_send, ms_recv, pan_send, pan_recv,
 ):
     r, c = lax.axis_index("row"), lax.axis_index("col")
     row_of = {d: lax.rem(r + d + nr, nr) for d in (-1, 0, 1)}
@@ -160,6 +160,7 @@
                 (pan_rows_hbm, pan_rows),
                 (ms_cols_hbm, ms_cols),
                 (ms_rows_hbm, ms_rows),
+                (gains_hbm, gains),
             )
         )
     ]
@@ -341,6 +342,10 @@
         copy.wait_send()
 
 
+def in_hbm(x):
+    return pltpu.with_memory_space_constraint(x, pltpu.HBM)
+
+
 def on_device(nr, nc, tables, ms, pan, gains):
     f32 = jnp.float32
     bf16 = jnp.bfloat16
@@ -348,7 +353,7 @@
     return pl.pallas_call(
         functools.partial(kernel, nr, nc),
         out_shape=jax.ShapeDtypeStruct((BANDS, ROWS, COLS), f32),
-        in_specs=[hbm, hbm, pl.BlockSpec(memory_space=pltpu.SMEM)] + [hbm] * 4,
+        in_specs=[hbm] * 7,
         out_specs=pl.BlockSpec(memory_space=pltpu.VMEM),
         scratch_shapes=[
             pltpu.VMEM((LROWS, nc * LCOLS), f32),
@@ -363,7 +368,8 @@
             pltpu.VMEM((3, ROWS, COLS), f32),
             pltpu.VMEM((BANDS * 64, 256), f32),
             pltpu.VMEM((BANDS * 64, COLS), f32),
-            pltpu.SemaphoreType.DMA((6,)),
+            pltpu.SMEM((3, BANDS), f32),
+            pltpu.SemaphoreType.DMA((7,)),
             pltpu.SemaphoreType.DMA,
             pltpu.SemaphoreType.DMA((3, nc)),
             pltpu.SemaphoreType.DMA((3, nc)),
@@ -373,7 +379,7 @@
         compiler_params=pltpu.CompilerParams(
             collective_id=0, has_side_effects=True, vmem_limit_bytes=32 * 1024 * 1024
         ),
-    )(ms, pan, gains.T, *[jnp.asarray(table) for table in tables])
+    )(in_hbm(ms), in_hbm(pan), in_hbm(gains.T), *[in_hbm(jnp.asarray(table)) for table in tables])
 
 
 def solution(mesh):

time: 29.1 us -> 21.5 us (0.74); the launches traced: 28.7 us -> 21.4 us
  local copies, waits for them, and re-layouts: 7.95 us -> 1.32 us
  Pallas kernels: 20.8 us -> 20.1 us
    unnamed x15 -> x1, local copies, waits for them, and re-layouts: 7.95 us -> 1.32 us
    pallas_call x1, Pallas kernels: 20.8 us -> 20.1 us  [on_device(): pl.pallas_call(functools.partial(kernel, nr, nc), out_shape=jax.ShapeDtyp...]
where the time goes in v2:
time: 21.5 us; the launch traced here: 21.4 us
  Pallas kernels  20.1 us (93%)
  local copies, waits for them, and re-layouts  1.32 us (6%)
    pallas_call x1, Pallas kernels, on_device(): pl.pallas_call(functools.partial(kernel, nr, nc), out_shape=jax.ShapeDtyp...  20.1 us
    unnamed x1, local copies, waits for them, and re-layouts  1.32 us

profile of v2, /device:TPU:0, one launch (start us, length us, event | category | flops | bytes accessed | tf_op | source)
XLA Modules:
  0.0 21.4 jit_solution(446152676135379337)
XLA Ops:
  0.0 20.1 %shard_map.73 = f32[8,128,512]{2,1,0:T(8,128)S(1)} custom-call(f32[1,32,1024]{2,1,0:T(8,128)} %ms_hbm.1, f32[128,512]{1,0:T(8,128)} %pan_hbm.1, f32[3,8]{1,0:T(4,128)} %bitcast.1, bf16[128,192]{1,0:T(8,128)(2,1)} %constant.8.clone.ms_rows_hbm, bf16[768,512]{1,0:T(8,128)(2,1)} %constant.9.clone.ms_cols_hbm, bf16[768,384]{1,0:T(8,128)(2,1)} %constant.10.clone.pan_cols_hbm, ...), custom_call_target="tpu_custom_call" | custom-call | tf_op jit(solution)/shard_map/pallas_call | solution.py:353
  20.1 1.3 %copy.9 = f32[8,128,512]{2,1,0:T(8,128)} copy(f32[8,128,512]{2,1,0:T(8,128)S(1)} %shard_map.73) | data formatting | bytes 4194304

commit v3 on v2

--- a/solution.py
+++ b/solution.py
@@ -127,45 +127,51 @@
     return high, low
 
 
-def kernel(
+def spread(
     nr, nc,
     ms_hbm, pan_hbm, gains_hbm, ms_rows_hbm, ms_cols_hbm, pan_cols_hbm, pan_rows_hbm,
-    out_ref,
+    terms, ysplit, ms_rows,
     ms_own, stage, mbuf, pan_ext, pstage, precv,
-    ms_rows, ms_cols, pan_cols, pan_rows,
-    pan_split, zbuf, qbuf, xsplit, ybuf,
+    ms_cols, pan_cols, pan_rows,
+    pan_roll, pan_split, zbuf, qbuf, xbuf,
     gains, load_sems, own_sem, ms_send, ms_recv, pan_send, pan_recv,
 ):
     r, c = lax.axis_index("row"), lax.axis_index("col")
+    half = nc // 2
     row_of = {d: lax.rem(r + d + nr, nr) for d in (-1, 0, 1)}
-    col_of = [lax.rem(c + k, nc) for k in range(nc)]
-
-    barrier = pltpu.get_barrier_semaphore()
-    for d in (-1, 0, 1):
-        for k in range(nc):
-            if d or k:
-                pl.semaphore_signal(
-                    barrier, inc=1, device_id=(row_of[d], col_of[k]), device_id_type=MESH
-                )
+    side, place = c // half, lax.rem(c, half)
+    halves = [lax.rem(side + a, 2) * half for a in range(2)]
+    col_of = {
+        (a, k): halves[a] + lax.rem(place + k, half) for a in range(2) for k in range(half)
+    }
 
     ms_load = pltpu.make_async_copy(ms_hbm.at[0], ms_own, load_sems.at[0])
     pan_load = pltpu.make_async_copy(
         pan_hbm, pan_ext.at[PAN_RIM : PAN_RIM + ROWS], load_sems.at[1]
     )
+    ms_load.start()
+    pan_load.start()
+
+    barrier = pltpu.get_barrier_semaphore()
+    for d in (-1, 0, 1):
+        for at, col in col_of.items():
+            if d or at != (0, 0):
+                pl.semaphore_signal(
+                    barrier, inc=1, device_id=(row_of[d], col), device_id_type=MESH
+                )
+
     table_loads = [
         pltpu.make_async_copy(source, target, load_sems.at[2 + i])
         for i, (source, target) in enumerate(
             (
                 (pan_cols_hbm, pan_cols),
                 (pan_rows_hbm, pan_rows),
+                (gains_hbm, gains),
                 (ms_cols_hbm, ms_cols),
                 (ms_rows_hbm, ms_rows),
-                (gains_hbm, gains),
             )
         )
     ]
-    ms_load.start()
-    pan_load.start()
     for load in table_loads:
         load.start()
 
@@ -195,24 +201,24 @@
         for step in range(0, count, 8):
             upper = PAN_RIM + first + step
             lower = upper + count
-            for side, column in ((0, 384), (1, 0)):
+            for way, column in ((0, 384), (1, 0)):
                 one = pan_ext[upper : upper + 8, column : column + 128]
                 two = pan_ext[lower : lower + 8, column : column + 128]
-                if side == 0:
+                if way == 0:
                     packed = jnp.where(lane < 64, pltpu.roll(one, 64, 1), two)
                 else:
                     packed = jnp.where(lane < 64, one, pltpu.roll(two, 64, 1))
-                pstage[side, at + step : at + step + 8] = packed
+                pstage[way, at + step : at + step + 8] = packed
 
     pl.semaphore_wait(barrier, 3 * nc - 1)
 
-    def remote(source, target, send_sem, recv_sem, d, k):
+    def remote(source, target, send_sem, recv_sem, d, col):
         return pltpu.make_async_remote_copy(
             src_ref=source,
             dst_ref=target,
             send_sem=send_sem,
             recv_sem=recv_sem,
-            device_id=(row_of[d], col_of[k % nc]),
+            device_id=(row_of[d], col),
             device_id_type=MESH,
         )
 
@@ -223,28 +229,34 @@
         (-1, pan_ext.at[own : own + PAN_RIM], pan_ext.at[own + ROWS : PAN_EXT]),
     ):
         at = len(pan_copies)
-        pan_copies.append(remote(source, target, pan_send.at[at], pan_recv.at[at], d, 0))
-    for side, k in ((0, 1), (1, -1)):
+        pan_copies.append(remote(source, target, pan_send.at[at], pan_recv.at[at], d, c))
+    for way, k in ((0, 1), (1, nc - 1)):
         for d, rows in ((0, slice(0, 64)), (1, slice(64, 88)), (-1, slice(88, 112))):
             at = len(pan_copies)
             pan_copies.append(
                 remote(
-                    pstage.at[side, rows], precv.at[side, rows],
-                    pan_send.at[at], pan_recv.at[at], d, k,
+                    pstage.at[way, rows], precv.at[way, rows],
+                    pan_send.at[at], pan_recv.at[at], d, lax.rem(c + k, nc),
                 )
             )
+    spans = {
+        0: (slice(0, 40), slice(24, 64)),
+        1: (slice(16, 40), slice(0, 24)),
+        -1: (slice(0, 24), slice(64, 88)),
+    }
     ms_copies = []
-    spans = {0: (slice(0, 40), slice(24, 64)), 1: (slice(16, 40), slice(0, 24)), -1: (slice(0, 24), slice(64, 88))}
-    for d in (0, 1, -1):
-        source, target = spans[d]
-        for k in range(nc):
-            if d or k:
-                ms_copies.append(
-                    remote(
-                        stage.at[col_of[k], source], mbuf.at[c, target],
-                        ms_send.at[d + 1, k], ms_recv.at[d + 1, c], d, k,
+    for a in (1, 0):
+        for k in range(half):
+            for d in (0, 1, -1):
+                if a or k or d:
+                    source, target = spans[d]
+                    ms_copies.append(
+                        remote(
+                            stage.at[col_of[a, k], source], mbuf.at[c, target],
+                            ms_send.at[d + 1, half * a + k], ms_recv.at[d + 1, c],
+                            d, col_of[a, k],
+                        )
                     )
-                )
     own_copy = pltpu.make_async_copy(stage.at[c], mbuf.at[c, 24:64], own_sem)
     for copy in pan_copies + ms_copies:
         copy.start()
@@ -255,13 +267,13 @@
     for step in range(0, PAN_EXT, 8):
         rows = slice(step, step + 8)
         if step < 48:
-            base, at, half = 0, 64, 24
+            base, at, count = 0, 64, 24
         elif step < 176:
-            base, at, half = 48, 0, 64
+            base, at, count = 48, 0, 64
         else:
-            base, at, half = 176, 88, 24
-        second = step - base >= half
-        inside = step - base - (half if second else 0)
+            base, at, count = 176, 88, 24
+        second = step - base >= count
+        inside = step - base - (count if second else 0)
         left = precv[0, at + inside : at + inside + 8]
         right = precv[1, at + inside : at + inside + 8]
         if second:
@@ -272,17 +284,14 @@
         tiles += [pltpu.roll(pan_ext[rows, 128 * t : 128 * t + 128], 64, 1) for t in range(4)]
         tiles += [right]
         for t in range(5):
-            value = jnp.where(lane < 64, tiles[t], tiles[t + 1])
-            high, low = parts_of(value)
-            pan_split[0, rows, 128 * t : 128 * t + 128] = high.astype(jnp.float32)
-            pan_split[1, rows, 128 * t : 128 * t + 128] = low.astype(jnp.float32)
+            pan_roll[rows, 128 * t : 128 * t + 128] = jnp.where(lane < 64, tiles[t], tiles[t + 1])
+    pan_split[0], pan_split[1] = parts_of(pan_roll[...])
 
     for load in table_loads:
         load.wait()
     for j in range(4):
         window = slice(128 * j, 128 * j + 256)
-        high = pan_split[0, :, window].astype(jnp.bfloat16)
-        low = pan_split[1, :, window].astype(jnp.bfloat16)
+        high, low = pan_split[0, :, window], pan_split[1, :, window]
         z = jnp.dot(
             jnp.concatenate([high, low, high], 1), pan_cols[...], preferred_element_type=jnp.float32
         )
@@ -293,53 +302,69 @@
     for level in range(3):
         qbuf[level] = jnp.dot(pan_rows[level], zbuf[level], preferred_element_type=jnp.float32)
 
+    def weigh(step, carry):
+        rows = pl.ds(pl.multiple_of(8 * step, 8), 8)
+        own_rows = pl.ds(pl.multiple_of(8 * step + PAN_RIM, 8), 8)
+        fields = [pan_ext[own_rows, :]] + [qbuf[level, rows, :] for level in range(3)]
+        for b in range(BANDS):
+            g1, g2, g3 = gains[0, b], gains[1, b], gains[2, b]
+            terms[b, rows, :] = (
+                g1 * fields[0] + (g2 - g1) * fields[1] + (g3 - g2) * fields[2] - g3 * fields[3]
+            )
+        return carry
+
+    lax.fori_loop(0, ROWS // 8, weigh, 0)
+
     own_copy.wait()
-    for d in (-1, 0, 1):
-        source, target = spans[d]
-        for k in range(nc):
-            if d or k:
-                remote(
-                    stage.at[col_of[k], source], mbuf.at[col_of[k], target],
-                    ms_send.at[d + 1, k], ms_recv.at[1 - d if d else 1, col_of[k]], d, k,
-                ).wait_recv()
-
-    def gather_band(b, carry):
-        for g, (main, rim, q) in enumerate(
-            (
-                (8, 0, 2), (16, 0, 3),
-                (24, 40, 0), (32, 40, 1), (48, 40, 2), (56, 40, 3),
-                (64, 80, 0), (72, 80, 1),
-            )
-        ):
-            rows = pl.ds(pl.multiple_of(64 * b, 64) + 8 * g, 8)
-            edge = mbuf[b, rim : rim + 8]
-            if q:
-                edge = pltpu.roll(edge, 128 - 32 * q, 1)
-            xsplit[rows, 0:128] = mbuf[b, main : main + 8]
-            xsplit[rows, 128:256] = edge
-        return carry
-
-    lax.fori_loop(0, BANDS, gather_band, 0)
-    high, low = parts_of(xsplit[...])
-    ybuf[...] = jnp.dot(
-        jnp.concatenate([high, low, high], 1), ms_cols[...], preferred_element_type=jnp.float32
-    )
-
-    def finish_band(b, carry):
-        g1, g2, g3 = gains[0, b], gains[1, b], gains[2, b]
-        high, low = parts_of(ybuf[pl.ds(pl.multiple_of(64 * b, 64), 64)])
-        total = jnp.dot(
-            ms_rows[...], jnp.concatenate([high, low, high], 0), preferred_element_type=jnp.float32
+    for a in range(2):
+        for k in range(half):
+            for d in (-1, 0, 1):
+                if a or k or d:
+                    source, target = spans[d]
+                    sender = col_of[a, k]
+                    remote(
+                        stage.at[sender, source], mbuf.at[sender, target],
+                        ms_send.at[d + 1, half * a + k], ms_recv.at[d + 1, sender],
+                        d, sender,
+                    ).wait_recv()
+        for k in range(half):
+            b = halves[a] + k
+            for g, (main, rim, q) in enumerate(
+                (
+                    (8, 0, 2), (16, 0, 3),
+                    (24, 40, 0), (32, 40, 1), (48, 40, 2), (56, 40, 3),
+                    (64, 80, 0), (72, 80, 1),
+                )
+            ):
+                rows = slice(64 * k + 8 * g, 64 * k + 8 * g + 8)
+                edge = mbuf[b, rim : rim + 8]
+                if q:
+                    edge = pltpu.roll(edge, 128 - 32 * q, 1)
+                xbuf[rows, 0:128] = mbuf[b, main : main + 8]
+                xbuf[rows, 128:256] = edge
+        high, low = parts_of(xbuf[...])
+        y = jnp.dot(
+            jnp.concatenate([high, low, high], 1), ms_cols[...], preferred_element_type=jnp.float32
         )
-        total += g1 * pan_ext[PAN_RIM : PAN_RIM + ROWS]
-        total += (g2 - g1) * qbuf[0] + (g3 - g2) * qbuf[1] - g3 * qbuf[2]
-        out_ref[b] = total
-        return carry
-
-    lax.fori_loop(0, BANDS, finish_band, 0)
+        high, low = parts_of(y)
+        for k in range(half):
+            ysplit[halves[a] + k, 0:64] = high[64 * k : 64 * k + 64]
+            ysplit[halves[a] + k, 64:128] = low[64 * k : 64 * k + 64]
 
     for copy in pan_copies + ms_copies:
         copy.wait_send()
+
+
+def finish(terms, ysplit, ms_rows, out_hbm, result, sems):
+    copies = []
+    for b in range(BANDS):
+        high = ysplit[b, 0:64]
+        column = jnp.concatenate([high, ysplit[b, 64:128], high], 0)
+        result[b] = terms[b] + jnp.dot(ms_rows[...], column, preferred_element_type=jnp.float32)
+        copies.append(pltpu.make_async_copy(result.at[b], out_hbm.at[b], sems.at[b]))
+        copies[-1].start()
+    for copy in copies:
+        copy.wait()
 
 
 def in_hbm(x):
@@ -350,11 +375,16 @@
     f32 = jnp.float32
     bf16 = jnp.bfloat16
     hbm = pl.BlockSpec(memory_space=pl.ANY)
-    return pl.pallas_call(
-        functools.partial(kernel, nr, nc),
-        out_shape=jax.ShapeDtypeStruct((BANDS, ROWS, COLS), f32),
+    vmem = pl.BlockSpec(memory_space=pltpu.VMEM)
+    shared = pl.pallas_call(
+        functools.partial(spread, nr, nc),
+        out_shape=[
+            pltpu.VMEM((BANDS, ROWS, COLS), f32),
+            pltpu.VMEM((BANDS, 128, COLS), bf16),
+            pltpu.VMEM(tables[0].shape, bf16),
+        ],
         in_specs=[hbm] * 7,
-        out_specs=pl.BlockSpec(memory_space=pltpu.VMEM),
+        out_specs=[vmem] * 3,
         scratch_shapes=[
             pltpu.VMEM((LROWS, nc * LCOLS), f32),
             pltpu.VMEM((nc, 40, 128), f32),
@@ -362,12 +392,12 @@
             pltpu.VMEM((PAN_EXT, COLS), f32),
             pltpu.VMEM((2, 112, 128), f32),
             pltpu.VMEM((2, 112, 128), f32),
-            *[pltpu.VMEM(table.shape, bf16) for table in tables],
-            pltpu.VMEM((2, PAN_EXT, COLS + 128), f32),
+            *[pltpu.VMEM(table.shape, bf16) for table in tables[1:]],
+            pltpu.VMEM((PAN_EXT, COLS + 128), f32),
+            pltpu.VMEM((2, PAN_EXT, COLS + 128), bf16),
             pltpu.VMEM((3, 3 * PAN_EXT, COLS), bf16),
             pltpu.VMEM((3, ROWS, COLS), f32),
-            pltpu.VMEM((BANDS * 64, 256), f32),
-            pltpu.VMEM((BANDS * 64, COLS), f32),
+            pltpu.VMEM((BANDS * 32, 256), f32),
             pltpu.SMEM((3, BANDS), f32),
             pltpu.SemaphoreType.DMA((7,)),
             pltpu.SemaphoreType.DMA,
@@ -380,6 +410,14 @@
             collective_id=0, has_side_effects=True, vmem_limit_bytes=32 * 1024 * 1024
         ),
     )(in_hbm(ms), in_hbm(pan), in_hbm(gains.T), *[in_hbm(jnp.asarray(table)) for table in tables])
+    return pl.pallas_call(
+        finish,
+        out_shape=jax.ShapeDtypeStruct((BANDS, ROWS, COLS), f32),
+        in_specs=[vmem] * 3,
+        out_specs=hbm,
+        scratch_shapes=[pltpu.VMEM((BANDS, ROWS, COLS), f32), pltpu.SemaphoreType.DMA((BANDS,))],
+        compiler_params=pltpu.CompilerParams(vmem_limit_bytes=16 * 1024 * 1024),
+    )(*shared)
 
 
 def solution(mesh):

time: 21.5 us -> 20.5 us (0.953)
  local copies, waits for them, and re-layouts: 1.32 us -> 0 us
  Pallas kernels: 20.1 us -> 20.4 us
    unnamed x1 -> x0, local copies, waits for them, and re-layouts: 1.32 us -> none
    pallas_call x1 -> x2, Pallas kernels: 20.1 us -> 20.4 us  [the longest x1 18.9 us: on_device(): pl.pallas_call(functools.partial(spread, nr, nc), out_shape=[pltpu.VMEM((...]
where the time goes in v3:
time: 20.5 us; the launch traced here: 20.4 us
  Pallas kernels  20.4 us (100%)
    pallas_call x1, Pallas kernels, on_device(): pl.pallas_call(functools.partial(spread, nr, nc), out_shape=[pltpu.VMEM((...  18.9 us
    pallas_call x1, Pallas kernels, on_device(): pl.pallas_call(finish, out_shape=jax.ShapeDtypeStruct((BANDS, ROWS, COLS)...  1.57 us

profile of v3, /device:TPU:0, one launch (start us, length us, event | category | flops | bytes accessed | tf_op | source)
XLA Modules:
  0.0 20.4 jit_solution(13821707765563487913)
XLA Ops:
  0.0 18.9 %shard_map.73 = (f32[8,128,512]{2,1,0:T(8,128)S(1)}, bf16[8,128,512]{2,1,0:T(8,128)(2,1)S(1)}, bf16[128,192]{1,0:T(8,128)(2,1)S(1)}) custom-call(f32[1,32,1024]{2,1,0:T(8,128)} %ms_hbm.1, f32[128,512]{1,0:T(8,128)} %pan_hbm.1, f32[3,8]{1,0:T(4,128)} %bitcast.1, bf16[128,192]{1,0:T(8,128)(2,1)} %constant.8.clone.ms_rows_hbm, ...), custom_call_target="tpu_custom_call" | custom-call | tf_op jit(solution)/shard_map/pallas_call | solution.py:379
  18.9 1.6 %shard_map.74 = f32[8,128,512]{2,1,0:T(8,128)} custom-call(f32[8,128,512]{2,1,0:T(8,128)S(1)} %get-tuple-element.8.terms, bf16[8,128,512]{2,1,0:T(8,128)(2,1)S(1)} %get-tuple-element.9.ysplit, bf16[128,192]{1,0:T(8,128)(2,1)S(1)} %get-tuple-element.10.ms_rows), custom_call_target="tpu_custom_call" | custom-call | tf_op jit(solution)/shard_map/pallas_call | solution.py:413

commit v4 on v3

--- a/solution.py
+++ b/solution.py
@@ -26,15 +26,18 @@
 
 ROWS, COLS = 128, 512
 LROWS, LCOLS = 32, 128
-PAN_RIM = 48
+PAN_RIM = 32
+PAN_SENT = 48
 PAN_EXT = ROWS + 2 * PAN_RIM
 MS_RIM = 16
 BANDS = 8
 
-
-def projection(level):
-    step = 2**level
-    rows = [{} for _ in range(8)]
+RIM_PIECES = [(3 * j, 3, (0, 26 * j), 3, 29) for j in range(4)]
+RIM_PIECES += [(12, 1, (0, 104), 3, 16), (12, 1, (1, 104), 16, 29)]
+
+
+def windows(level):
+    found = []
     for tree in range(2):
         taps = TAPS if tree == 0 else TAPS[::-1]
         cascade, shift = [1.0], 0
@@ -44,11 +47,17 @@
                 for j, tap in enumerate(taps):
                     longer[i + j * 2**lev] += value * tap
             cascade, shift = longer, shift + (3 + tree) * 2**lev
-        span = len(cascade)
+        found.append((2**level, shift, cascade))
+    return found
+
+
+def projection(level):
+    rows = [{} for _ in range(8)]
+    for step, shift, cascade in windows(level):
         for m in range(8):
             for k in range(-64, 64):
                 at = m - step * k + shift
-                if 0 <= at < span:
+                if 0 <= at < len(cascade):
                     for i, value in enumerate(cascade):
                         offset = step * k - shift + i - m
                         rows[m][offset] = rows[m].get(offset, 0.0) + 0.5 * cascade[at] * value
@@ -87,13 +96,47 @@
     rows = projection(level)
     for m in range(outs):
         for offset, weight in rows[m % 8].items():
-            matrix[m, m + offset - start] = weight
+            if 0 <= m + offset - start < ins:
+                matrix[m, m + offset - start] = weight
     return matrix
 
 
-def ms_matrix(outs, lows):
+def straddling(edge):
+    found = []
+    for level in (1, 2, 3):
+        for step, shift, cascade in windows(level):
+            for k in range(-64, 128):
+                first = step * k - shift
+                if first < edge < first + len(cascade):
+                    found.append((level, first, cascade))
+    return found
+
+
+def row_tables():
+    above, below = straddling(0), straddling(ROWS)
+    down = np.zeros((PAN_RIM, PAN_SENT))
+    up = np.zeros((PAN_RIM, PAN_SENT))
+    merged = np.zeros((3, ROWS, PAN_EXT))
+    for level in (1, 2, 3):
+        merged[level - 1, :, PAN_RIM : PAN_RIM + ROWS] = pan_matrix(level, ROWS, ROWS, 0)
+    for at, (level, first, cascade) in enumerate(above):
+        for i, weight in enumerate(cascade):
+            if first + i < 0:
+                down[at, first + i + PAN_SENT] = weight
+            else:
+                merged[level - 1, first + i, at] = 0.5 * weight
+    for at, (level, first, cascade) in enumerate(below):
+        for i, weight in enumerate(cascade):
+            if first + i >= ROWS:
+                up[at, first + i - ROWS] = weight
+            else:
+                merged[level - 1, first + i, PAN_RIM + ROWS + at] = 0.5 * weight
+    return down, up, merged
+
+
+def ms_matrix(outs, ins, lows):
     place = {low: at for at, low in lows}
-    matrix = np.zeros((outs, max(at for at, _ in lows) + 1))
+    matrix = np.zeros((outs, ins))
     rows = upsampled_projection()
     for m in range(outs):
         for low, weight in rows[m % 8].items():
@@ -102,23 +145,31 @@
 
 
 def make_tables():
-    high, low = split_parts(ms_matrix(ROWS, [(i, i - MS_RIM) for i in range(LROWS + 2 * MS_RIM)]))
-    ms_rows = np.concatenate([high, high, low], 1)
+    ms_rows = []
+    for odd in (0, 1):
+        inner, outer = (-16, 32) if odd else (32, -13)
+        lows = [(i, i) for i in range(LROWS)]
+        lows += [(LROWS + i, inner + i) for i in range(16)]
+        lows += [(LROWS + 19 + i, outer + i) for i in range(13)]
+        high, low = split_parts(ms_matrix(ROWS, 64, lows))
+        ms_rows.append(np.concatenate([high, high, low], 1))
     lows = [(i, i) for i in range(LCOLS)]
     lows += [(LCOLS + i, i - MS_RIM) for i in range(MS_RIM)]
     lows += [(LCOLS + MS_RIM + i, LCOLS + i) for i in range(MS_RIM)]
-    matrix = ms_matrix(COLS, lows)
-    matrix = np.pad(matrix, ((0, 0), (0, 256 - matrix.shape[1]))).T
-    high, low = split_parts(matrix)
+    high, low = split_parts(ms_matrix(COLS, 256, lows).T)
     ms_cols = np.concatenate([high, high, low], 0)
     matrix = np.concatenate([pan_matrix(level, 128, 256, -64) for level in (1, 2, 3)], 0).T
     high, low = split_parts(matrix)
     pan_cols = np.concatenate([high, high, low], 0)
-    pan_rows = []
-    for level in (1, 2, 3):
-        high, low = split_parts(pan_matrix(level, ROWS, PAN_EXT, -PAN_RIM))
+    sums, pan_rows = [], []
+    down, up, merged = row_tables()
+    for matrix in (down, up):
+        high, low = split_parts(matrix)
+        sums.append(np.concatenate([high, high, low], 1))
+    for level in range(3):
+        high, low = split_parts(merged[level])
         pan_rows.append(np.concatenate([high, high, low], 1))
-    return ms_rows, ms_cols, pan_cols, np.stack(pan_rows)
+    return np.stack(ms_rows), ms_cols, pan_cols, np.stack(pan_rows), np.stack(sums)
 
 
 def parts_of(x):
@@ -129,10 +180,10 @@
 
 def spread(
     nr, nc,
-    ms_hbm, pan_hbm, gains_hbm, ms_rows_hbm, ms_cols_hbm, pan_cols_hbm, pan_rows_hbm,
+    ms_hbm, pan_hbm, gains_hbm, ms_rows_hbm, ms_cols_hbm, pan_cols_hbm, pan_rows_hbm, sums_hbm,
     terms, ysplit, ms_rows,
-    ms_own, stage, mbuf, pan_ext, pstage, precv,
-    ms_cols, pan_cols, pan_rows,
+    ms_own, stage, ostage, mbuf, obuf, pan_ext, psums, pstage, precv,
+    ms_cols, pan_cols, pan_rows, sums,
     pan_roll, pan_split, zbuf, qbuf, xbuf,
     gains, load_sems, own_sem, ms_send, ms_recv, pan_send, pan_recv,
 ):
@@ -149,16 +200,25 @@
     pan_load = pltpu.make_async_copy(
         pan_hbm, pan_ext.at[PAN_RIM : PAN_RIM + ROWS], load_sems.at[1]
     )
+    sums_load = pltpu.make_async_copy(sums_hbm, sums, load_sems.at[7])
     ms_load.start()
     pan_load.start()
+    sums_load.start()
+
+    odd = lax.rem(r, 2)
+    inner = lax.rem(r + 1 - 2 * odd + nr, nr)
+    outer = lax.rem(r - 1 + 2 * odd + nr, nr)
 
     barrier = pltpu.get_barrier_semaphore()
-    for d in (-1, 0, 1):
-        for at, col in col_of.items():
-            if d or at != (0, 0):
-                pl.semaphore_signal(
-                    barrier, inc=1, device_id=(row_of[d], col), device_id_type=MESH
-                )
+    for col in col_of.values():
+        pl.semaphore_signal(barrier, inc=1, device_id=(outer, col), device_id_type=MESH)
+    for at, col in col_of.items():
+        if at != (0, 0):
+            pl.semaphore_signal(barrier, inc=1, device_id=(r, col), device_id_type=MESH)
+    for k in (0, 1, nc - 1):
+        pl.semaphore_signal(
+            barrier, inc=1, device_id=(inner, lax.rem(c + k, nc)), device_id_type=MESH
+        )
 
     table_loads = [
         pltpu.make_async_copy(source, target, load_sems.at[2 + i])
@@ -168,7 +228,7 @@
                 (pan_rows_hbm, pan_rows),
                 (gains_hbm, gains),
                 (ms_cols_hbm, ms_cols),
-                (ms_rows_hbm, ms_rows),
+                (ms_rows_hbm.at[odd], ms_rows),
             )
         )
     ]
@@ -176,6 +236,7 @@
         load.start()
 
     lane = lax.broadcasted_iota(jnp.int32, (8, 128), 1)
+    sublane = lax.broadcasted_iota(jnp.int32, (8, 128), 0)
 
     ms_load.wait()
     for dest in range(nc):
@@ -196,82 +257,137 @@
             rim = both if rim is None else jnp.where(lane < 32 * q, rim, both)
         stage[dest, 16:24] = rim
 
+    for way in range(2):
+
+        @pl.when(odd == way)
+        def _():
+            for dest in range(nc):
+                tile = slice(128 * dest, 128 * dest + 128)
+                if way:
+                    upper, lower = ms_own[16:24, tile], ms_own[24:32, tile]
+                else:
+                    upper = pltpu.roll(ms_own[0:8, tile], 3, 0)
+                    lower = jnp.where(sublane < 3, upper, pltpu.roll(ms_own[8:16, tile], 3, 0))
+                rim = stage[dest, 16:24]
+                for i, count, at, first, last in RIM_PIECES:
+                    row = i + 19 * way
+                    while count:
+                        q, sub = row // 8, row % 8
+                        now = min(count, 8 - sub)
+                        moved = pltpu.roll(rim, (at[0] - sub) % 8, 0)
+                        moved = pltpu.roll(moved, (at[1] - 32 * q - first) % 128, 1)
+                        inside = (sublane >= at[0]) & (sublane < at[0] + now)
+                        inside &= (lane >= at[1]) & (lane < at[1] + last - first)
+                        upper = jnp.where(inside, moved, upper)
+                        row, count, at = row + now, count - now, (at[0] + now, at[1])
+                ostage[dest, 0:8] = upper
+                ostage[dest, 8:16] = lower
+
     pan_load.wait()
-    for at, (first, count) in ((0, (0, 64)), (64, (80, 24)), (88, (0, 24))):
+    sums_load.wait()
+    for way, first in ((0, PAN_RIM + ROWS - PAN_SENT), (1, PAN_RIM)):
+        high, low = parts_of(pan_ext[first : first + PAN_SENT])
+        psums[way] = jnp.dot(
+            sums[way], jnp.concatenate([high, low, high], 0), preferred_element_type=jnp.float32
+        )
+    for at, source, first, count in (
+        (0, pan_ext, PAN_RIM, 64), (64, psums.at[0], 0, 16), (80, psums.at[1], 0, 16)
+    ):
         for step in range(0, count, 8):
-            upper = PAN_RIM + first + step
+            upper = first + step
             lower = upper + count
             for way, column in ((0, 384), (1, 0)):
-                one = pan_ext[upper : upper + 8, column : column + 128]
-                two = pan_ext[lower : lower + 8, column : column + 128]
+                one = source[upper : upper + 8, column : column + 128]
+                two = source[lower : lower + 8, column : column + 128]
                 if way == 0:
                     packed = jnp.where(lane < 64, pltpu.roll(one, 64, 1), two)
                 else:
                     packed = jnp.where(lane < 64, one, pltpu.roll(two, 64, 1))
                 pstage[way, at + step : at + step + 8] = packed
 
-    pl.semaphore_wait(barrier, 3 * nc - 1)
-
-    def remote(source, target, send_sem, recv_sem, d, col):
+    pl.semaphore_wait(barrier, 2 * nc + 2)
+
+    def remote(source, target, send_sem, recv_sem, row, col):
         return pltpu.make_async_remote_copy(
             src_ref=source,
             dst_ref=target,
             send_sem=send_sem,
             recv_sem=recv_sem,
-            device_id=(row_of[d], col),
+            device_id=(row, col),
             device_id_type=MESH,
         )
 
     pan_copies = []
-    own = PAN_RIM
     for d, source, target in (
-        (1, pan_ext.at[own + ROWS - PAN_RIM : own + ROWS], pan_ext.at[0:PAN_RIM]),
-        (-1, pan_ext.at[own : own + PAN_RIM], pan_ext.at[own + ROWS : PAN_EXT]),
+        (1, psums.at[0], pan_ext.at[0:PAN_RIM]),
+        (-1, psums.at[1], pan_ext.at[PAN_RIM + ROWS : PAN_EXT]),
     ):
         at = len(pan_copies)
-        pan_copies.append(remote(source, target, pan_send.at[at], pan_recv.at[at], d, c))
+        pan_copies.append(remote(source, target, pan_send.at[at], pan_recv.at[at], row_of[d], c))
     for way, k in ((0, 1), (1, nc - 1)):
-        for d, rows in ((0, slice(0, 64)), (1, slice(64, 88)), (-1, slice(88, 112))):
+        for d, rows in ((0, slice(0, 64)), (1, slice(64, 80)), (-1, slice(80, 96))):
             at = len(pan_copies)
             pan_copies.append(
                 remote(
                     pstage.at[way, rows], precv.at[way, rows],
-                    pan_send.at[at], pan_recv.at[at], d, lax.rem(c + k, nc),
+                    pan_send.at[at], pan_recv.at[at], row_of[d], lax.rem(c + k, nc),
                 )
             )
-    spans = {
-        0: (slice(0, 40), slice(24, 64)),
-        1: (slice(16, 40), slice(0, 24)),
-        -1: (slice(0, 24), slice(64, 88)),
-    }
-    ms_copies = []
+    def rows_of(first, count):
+        return pl.ds(pl.multiple_of(first, 8), count)
+
+    same_copies, outer_copies = [], []
     for a in (1, 0):
         for k in range(half):
-            for d in (0, 1, -1):
-                if a or k or d:
-                    source, target = spans[d]
-                    ms_copies.append(
-                        remote(
-                            stage.at[col_of[a, k], source], mbuf.at[c, target],
-                            ms_send.at[d + 1, half * a + k], ms_recv.at[d + 1, c],
-                            d, col_of[a, k],
-                        )
+            col = col_of[a, k]
+            at = half * a + k
+            if a or k:
+                same_copies.append(
+                    remote(
+                        stage.at[col], mbuf.at[c, 0:40],
+                        ms_send.at[0, at], ms_recv.at[0, c], r, col,
                     )
-    own_copy = pltpu.make_async_copy(stage.at[c], mbuf.at[c, 24:64], own_sem)
-    for copy in pan_copies + ms_copies:
+                )
+            outer_copies.append(
+                remote(
+                    ostage.at[col], obuf.at[c],
+                    ms_send.at[1, at], ms_recv.at[1, c], outer, col,
+                )
+            )
+    own_copy = pltpu.make_async_copy(stage.at[c], mbuf.at[c, 0:40], own_sem)
+    own_copy.start()
+    for copy in same_copies + pan_copies + outer_copies:
         copy.start()
-    own_copy.start()
+
+    own_copy.wait()
+    inner_copies = []
+    for a in (0, 1):
+        for k in range(half):
+            if a or k:
+                sender = col_of[a, k]
+                remote(
+                    stage.at[sender], mbuf.at[sender, 0:40],
+                    ms_send.at[0, half * a + k], ms_recv.at[0, sender], r, sender,
+                ).wait_recv()
+        bands = pl.ds(halves[a], half)
+        inner_copies.append(
+            remote(
+                mbuf.at[bands, rows_of(16 - 16 * odd, 24)], mbuf.at[bands, 40:64],
+                ms_send.at[2, a], ms_recv.at[2, a], inner, c,
+            )
+        )
+        inner_copies[-1].start()
 
     for copy in pan_copies:
         copy.wait_recv()
     for step in range(0, PAN_EXT, 8):
         rows = slice(step, step + 8)
-        if step < 48:
-            base, at, count = 0, 64, 24
-        elif step < 176:
-            base, at, count = 48, 0, 64
+        if step < PAN_RIM:
+            base, at, count = 0, 64, 16
+        elif step < PAN_RIM + ROWS:
+            base, at, count = PAN_RIM, 0, 64
         else:
-            base, at, count = 176, 88, 24
+            base, at, count = PAN_RIM + ROWS, 80, 16
         second = step - base >= count
         inside = step - base - (count if second else 0)
         left = precv[0, at + inside : at + inside + 8]
@@ -315,33 +431,40 @@
 
     lax.fori_loop(0, ROWS // 8, weigh, 0)
 
-    own_copy.wait()
     for a in range(2):
+        inner_copies[a].wait_recv()
         for k in range(half):
-            for d in (-1, 0, 1):
-                if a or k or d:
-                    source, target = spans[d]
-                    sender = col_of[a, k]
-                    remote(
-                        stage.at[sender, source], mbuf.at[sender, target],
-                        ms_send.at[d + 1, half * a + k], ms_recv.at[d + 1, sender],
-                        d, sender,
-                    ).wait_recv()
+            sender = col_of[a, k]
+            remote(
+                ostage.at[sender], obuf.at[sender],
+                ms_send.at[1, half * a + k], ms_recv.at[1, sender], outer, sender,
+            ).wait_recv()
         for k in range(half):
             b = halves[a] + k
-            for g, (main, rim, q) in enumerate(
-                (
-                    (8, 0, 2), (16, 0, 3),
-                    (24, 40, 0), (32, 40, 1), (48, 40, 2), (56, 40, 3),
-                    (64, 80, 0), (72, 80, 1),
-                )
-            ):
+            parts = [(mbuf[b, m : m + 8], mbuf[b, 16:24], 32 * q) for q, m in enumerate((0, 8, 24, 32))]
+            rim = mbuf[b, rows_of(56 - 16 * odd, 8)]
+            for q in range(2):
+                parts.append((mbuf[b, rows_of(40 + 8 * odd + 8 * q, 8)], rim, 32 * q + 64 * odd))
+            for g, (main, rim, at) in enumerate(parts):
                 rows = slice(64 * k + 8 * g, 64 * k + 8 * g + 8)
-                edge = mbuf[b, rim : rim + 8]
-                if q:
-                    edge = pltpu.roll(edge, 128 - 32 * q, 1)
-                xbuf[rows, 0:128] = mbuf[b, main : main + 8]
-                xbuf[rows, 128:256] = edge
+                xbuf[rows, 0:128] = main
+                xbuf[rows, 128:256] = pltpu.roll(rim, lax.rem(128 - at, 128), 1)
+            upper, lower = obuf[b, 0:8], obuf[b, 8:16]
+            rims = [upper, lower]
+            for i, count, at, first, last in RIM_PIECES:
+                moved = pltpu.roll(upper, (i + 3 - at[0]) % 8, 0)
+                moved = pltpu.roll(moved, (first - at[1]) % 128, 1)
+                for v in range(2):
+                    low, high = i + 3 - 8 * v, i + 3 + count - 8 * v
+                    if low < 8 and high > 0:
+                        inside = (sublane >= low) & (sublane < high)
+                        if last - first < 26:
+                            inside &= (lane >= first) & (lane < last)
+                        rims[v] = jnp.where(inside, moved, rims[v])
+            for v, main in enumerate((upper, lower)):
+                rows = slice(64 * k + 48 + 8 * v, 64 * k + 56 + 8 * v)
+                xbuf[rows, 0:128] = main
+                xbuf[rows, 128:256] = rims[v]
         high, low = parts_of(xbuf[...])
         y = jnp.dot(
             jnp.concatenate([high, low, high], 1), ms_cols[...], preferred_element_type=jnp.float32
@@ -351,7 +474,7 @@
             ysplit[halves[a] + k, 0:64] = high[64 * k : 64 * k + 64]
             ysplit[halves[a] + k, 64:128] = low[64 * k : 64 * k + 64]
 
-    for copy in pan_copies + ms_copies:
+    for copy in same_copies + pan_copies + outer_copies + inner_copies:
         copy.wait_send()
 
 
@@ -381,17 +504,20 @@
         out_shape=[
             pltpu.VMEM((BANDS, ROWS, COLS), f32),
             pltpu.VMEM((BANDS, 128, COLS), bf16),
-            pltpu.VMEM(tables[0].shape, bf16),
+            pltpu.VMEM(tables[0].shape[1:], bf16),
         ],
-        in_specs=[hbm] * 7,
+        in_specs=[hbm] * 8,
         out_specs=[vmem] * 3,
         scratch_shapes=[
             pltpu.VMEM((LROWS, nc * LCOLS), f32),
             pltpu.VMEM((nc, 40, 128), f32),
-            pltpu.VMEM((BANDS, 88, 128), f32),
+            pltpu.VMEM((nc, 16, 128), f32),
+            pltpu.VMEM((BANDS, 64, 128), f32),
+            pltpu.VMEM((BANDS, 16, 128), f32),
             pltpu.VMEM((PAN_EXT, COLS), f32),
-            pltpu.VMEM((2, 112, 128), f32),
-            pltpu.VMEM((2, 112, 128), f32),
+            pltpu.VMEM((2, PAN_RIM, COLS), f32),
+            pltpu.VMEM((2, 96, 128), f32),
+            pltpu.VMEM((2, 96, 128), f32),
             *[pltpu.VMEM(table.shape, bf16) for table in tables[1:]],
             pltpu.VMEM((PAN_EXT, COLS + 128), f32),
             pltpu.VMEM((2, PAN_EXT, COLS + 128), bf16),
@@ -399,7 +525,7 @@
             pltpu.VMEM((3, ROWS, COLS), f32),
             pltpu.VMEM((BANDS * 32, 256), f32),
             pltpu.SMEM((3, BANDS), f32),
-            pltpu.SemaphoreType.DMA((7,)),
+            pltpu.SemaphoreType.DMA((8,)),
             pltpu.SemaphoreType.DMA,
             pltpu.SemaphoreType.DMA((3, nc)),
             pltpu.SemaphoreType.DMA((3, nc)),

time: 20.5 us -> 19.4 us (0.946)
  Pallas kernels: 20.4 us -> 19.2 us
    pallas_call x1, Pallas kernels: 18.9 us -> 17.7 us  [on_device(): pl.pallas_call(functools.partial(spread, nr, nc), out_shape=[pltpu.VMEM((...]
where the time goes in v4:
time: 19.4 us; the launch traced here: 19.2 us
  Pallas kernels  19.2 us (99%)
    pallas_call x1, Pallas kernels, on_device(): pl.pallas_call(functools.partial(spread, nr, nc), out_shape=[pltpu.VMEM((...  17.7 us
    pallas_call x1, Pallas kernels, on_device(): pl.pallas_call(finish, out_shape=jax.ShapeDtypeStruct((BANDS, ROWS, COLS)...  1.57 us

profile of v4, /device:TPU:0, one launch (start us, length us, event | category | flops | bytes accessed | tf_op | source)
XLA Modules:
  0.0 19.2 jit_solution(9215512566138042844)
XLA Ops:
  0.0 17.7 %shard_map.82 = (f32[8,128,512]{2,1,0:T(8,128)S(1)}, bf16[8,128,512]{2,1,0:T(8,128)(2,1)S(1)}, bf16[128,192]{1,0:T(8,128)(2,1)S(1)}) custom-call(f32[1,32,1024]{2,1,0:T(8,128)} %ms_hbm.1, f32[128,512]{1,0:T(8,128)} %pan_hbm.1, f32[3,8]{1,0:T(4,128)} %bitcast.1, bf16[2,128,192]{2,1,0:T(8,128)(2,1)} %constant.10.clone.ms_rows_hbm, ...), custom_call_target="tpu_custom_call" | custom-call | tf_op jit(solution)/shard_map/pallas_call | solution.py:502
  17.7 1.6 %shard_map.83 = f32[8,128,512]{2,1,0:T(8,128)} custom-call(f32[8,128,512]{2,1,0:T(8,128)S(1)} %get-tuple-element.8.terms, bf16[8,128,512]{2,1,0:T(8,128)(2,1)S(1)} %get-tuple-element.9.ysplit, bf16[128,192]{1,0:T(8,128)(2,1)S(1)} %get-tuple-element.10.ms_rows), custom_call_target="tpu_custom_call" | custom-call | tf_op jit(solution)/shard_map/pallas_call | solution.py:539

commit v5 on v4

--- a/solution.py
+++ b/solution.py
@@ -118,19 +118,19 @@
     up = np.zeros((PAN_RIM, PAN_SENT))
     merged = np.zeros((3, ROWS, PAN_EXT))
     for level in (1, 2, 3):
-        merged[level - 1, :, PAN_RIM : PAN_RIM + ROWS] = pan_matrix(level, ROWS, ROWS, 0)
+        merged[level - 1, :, :ROWS] = pan_matrix(level, ROWS, ROWS, 0)
     for at, (level, first, cascade) in enumerate(above):
         for i, weight in enumerate(cascade):
             if first + i < 0:
                 down[at, first + i + PAN_SENT] = weight
             else:
-                merged[level - 1, first + i, at] = 0.5 * weight
+                merged[level - 1, first + i, ROWS + at] = 0.5 * weight
     for at, (level, first, cascade) in enumerate(below):
         for i, weight in enumerate(cascade):
             if first + i >= ROWS:
                 up[at, first + i - ROWS] = weight
             else:
-                merged[level - 1, first + i, PAN_RIM + ROWS + at] = 0.5 * weight
+                merged[level - 1, first + i, ROWS + PAN_RIM + at] = 0.5 * weight
     return down, up, merged
 
 
@@ -178,14 +178,21 @@
     return high, low
 
 
+def rolled(tiles, beside):
+    left = lax.broadcasted_iota(jnp.int32, beside.shape, 1) < 64
+    turned = [pltpu.roll(tile, 64, 1) for tile in tiles]
+    firsts, seconds = [beside] + turned, turned + [beside]
+    return [jnp.where(left, one, two) for one, two in zip(firsts, seconds)]
+
+
 def spread(
     nr, nc,
     ms_hbm, pan_hbm, gains_hbm, ms_rows_hbm, ms_cols_hbm, pan_cols_hbm, pan_rows_hbm, sums_hbm,
     terms, ysplit, ms_rows,
-    ms_own, stage, ostage, mbuf, obuf, pan_ext, psums, pstage, precv,
+    ms_own, stage, ostage, mbuf, obuf, pan_own, psums, pan_above_below, pstage, precv, cstage, crecv,
     ms_cols, pan_cols, pan_rows, sums,
-    pan_roll, pan_split, zbuf, qbuf, xbuf,
-    gains, load_sems, own_sem, ms_send, ms_recv, pan_send, pan_recv,
+    pan_split, zbuf, qbuf, xbuf,
+    gains, load_sems, ms_recv, pan_recv, send_sems,
 ):
     r, c = lax.axis_index("row"), lax.axis_index("col")
     half = nc // 2
@@ -197,9 +204,7 @@
     }
 
     ms_load = pltpu.make_async_copy(ms_hbm.at[0], ms_own, load_sems.at[0])
-    pan_load = pltpu.make_async_copy(
-        pan_hbm, pan_ext.at[PAN_RIM : PAN_RIM + ROWS], load_sems.at[1]
-    )
+    pan_load = pltpu.make_async_copy(pan_hbm, pan_own, load_sems.at[1])
     sums_load = pltpu.make_async_copy(sums_hbm, sums, load_sems.at[7])
     ms_load.start()
     pan_load.start()
@@ -283,28 +288,6 @@
                 ostage[dest, 0:8] = upper
                 ostage[dest, 8:16] = lower
 
-    pan_load.wait()
-    sums_load.wait()
-    for way, first in ((0, PAN_RIM + ROWS - PAN_SENT), (1, PAN_RIM)):
-        high, low = parts_of(pan_ext[first : first + PAN_SENT])
-        psums[way] = jnp.dot(
-            sums[way], jnp.concatenate([high, low, high], 0), preferred_element_type=jnp.float32
-        )
-    for at, source, first, count in (
-        (0, pan_ext, PAN_RIM, 64), (64, psums.at[0], 0, 16), (80, psums.at[1], 0, 16)
-    ):
-        for step in range(0, count, 8):
-            upper = first + step
-            lower = upper + count
-            for way, column in ((0, 384), (1, 0)):
-                one = source[upper : upper + 8, column : column + 128]
-                two = source[lower : lower + 8, column : column + 128]
-                if way == 0:
-                    packed = jnp.where(lane < 64, pltpu.roll(one, 64, 1), two)
-                else:
-                    packed = jnp.where(lane < 64, one, pltpu.roll(two, 64, 1))
-                pstage[way, at + step : at + step + 8] = packed
-
     pl.semaphore_wait(barrier, 2 * nc + 2)
 
     def remote(source, target, send_sem, recv_sem, row, col):
@@ -317,111 +300,132 @@
             device_id_type=MESH,
         )
 
-    pan_copies = []
-    for d, source, target in (
-        (1, psums.at[0], pan_ext.at[0:PAN_RIM]),
-        (-1, psums.at[1], pan_ext.at[PAN_RIM + ROWS : PAN_EXT]),
-    ):
-        at = len(pan_copies)
-        pan_copies.append(remote(source, target, pan_send.at[at], pan_recv.at[at], row_of[d], c))
-    for way, k in ((0, 1), (1, nc - 1)):
-        for d, rows in ((0, slice(0, 64)), (1, slice(64, 80)), (-1, slice(80, 96))):
-            at = len(pan_copies)
-            pan_copies.append(
-                remote(
-                    pstage.at[way, rows], precv.at[way, rows],
-                    pan_send.at[at], pan_recv.at[at], row_of[d], lax.rem(c + k, nc),
-                )
-            )
     def rows_of(first, count):
         return pl.ds(pl.multiple_of(first, 8), count)
 
-    same_copies, outer_copies = [], []
     for a in (1, 0):
         for k in range(half):
+            if a or k:
+                col = col_of[a, k]
+                remote(
+                    stage.at[col], mbuf.at[c, 0:40], send_sems.at[0], ms_recv.at[0, a], r, col
+                ).start()
+    mbuf[c, 0:40] = stage[c]
+
+    pan_load.wait()
+    sums_load.wait()
+    for way, rows in ((0, slice(ROWS - PAN_SENT, ROWS)), (1, slice(0, PAN_SENT))):
+        high, low = parts_of(pan_own[rows])
+        psums[way] = jnp.dot(
+            sums[way], jnp.concatenate([high, low, high], 0), preferred_element_type=jnp.float32
+        )
+    for source, at in ((pan_own, pstage), (psums.at[0], cstage.at[0]), (psums.at[1], cstage.at[1])):
+        half_rows = source.shape[0] // 2
+        left = lax.broadcasted_iota(jnp.int32, (half_rows, 128), 1) < 64
+        last, first = source[:, 384:512], source[:, 0:128]
+        at[0] = jnp.where(left, pltpu.roll(last[:half_rows], 64, 1), last[half_rows:])
+        at[1] = jnp.where(left, first[:half_rows], pltpu.roll(first[half_rows:], 64, 1))
+
+    def send_outer(a):
+        for k in range(half):
             col = col_of[a, k]
-            at = half * a + k
-            if a or k:
-                same_copies.append(
-                    remote(
-                        stage.at[col], mbuf.at[c, 0:40],
-                        ms_send.at[0, at], ms_recv.at[0, c], r, col,
-                    )
-                )
-            outer_copies.append(
-                remote(
-                    ostage.at[col], obuf.at[c],
-                    ms_send.at[1, at], ms_recv.at[1, c], outer, col,
-                )
+            remote(
+                ostage.at[col], obuf.at[c], send_sems.at[1], ms_recv.at[1, a], outer, col
+            ).start()
+
+    send_outer(1)
+    for way, d in ((0, 1), (1, -1)):
+        remote(
+            psums.at[way], pan_above_below.at[way],
+            send_sems.at[3], pan_recv.at[0], row_of[d], c,
+        ).start()
+    for side_at, k in ((0, 1), (1, nc - 1)):
+        beside = lax.rem(c + k, nc)
+        remote(
+            pstage.at[side_at], precv.at[side_at], send_sems.at[4], pan_recv.at[1], r, beside
+        ).start()
+        for way, d in ((0, 1), (1, -1)):
+            remote(
+                cstage.at[way, side_at], crecv.at[way, side_at],
+                send_sems.at[5], pan_recv.at[2], row_of[d], beside,
+            ).start()
+    send_outer(0)
+
+    for a in (0, 1):
+        arrived = mbuf.at[0 : half - 1 + a, 0:40]
+        remote(arrived, arrived, send_sems.at[0], ms_recv.at[0, a], r, col_of[0, 1]).wait_recv()
+        bands = pl.ds(halves[a], half)
+        remote(
+            mbuf.at[bands, rows_of(16 - 16 * odd, 24)], mbuf.at[bands, 40:64],
+            send_sems.at[2], ms_recv.at[2, a], inner, c,
+        ).start()
+
+    def unpacked(packed):
+        left = lax.broadcasted_iota(jnp.int32, packed.shape[1:], 1) < 64
+        one, two = packed[0], packed[1]
+        return jnp.concatenate(
+            [
+                jnp.where(left, one, pltpu.roll(two, 64, 1)),
+                jnp.where(left, pltpu.roll(one, 64, 1), two),
+            ],
+            0,
+        )
+
+    def pan_columns(rows, count, tiles, ends):
+        for t, tile in enumerate(rolled(tiles, ends)):
+            for part, value in enumerate(parts_of(tile)):
+                pan_split[part, rows : rows + count, 128 * t : 128 * t + 128] = value
+        for j in range(4):
+            window = slice(128 * j, 128 * j + 256)
+            high, low = (pan_split[part, rows : rows + count, window] for part in range(2))
+            z = jnp.dot(
+                jnp.concatenate([high, low, high], 1),
+                pan_cols[...],
+                preferred_element_type=jnp.float32,
             )
-    own_copy = pltpu.make_async_copy(stage.at[c], mbuf.at[c, 0:40], own_sem)
-    own_copy.start()
-    for copy in same_copies + pan_copies + outer_copies:
-        copy.start()
-
-    own_copy.wait()
-    inner_copies = []
-    for a in (0, 1):
-        for k in range(half):
-            if a or k:
-                sender = col_of[a, k]
-                remote(
-                    stage.at[sender], mbuf.at[sender, 0:40],
-                    ms_send.at[0, half * a + k], ms_recv.at[0, sender], r, sender,
-                ).wait_recv()
-        bands = pl.ds(halves[a], half)
-        inner_copies.append(
-            remote(
-                mbuf.at[bands, rows_of(16 - 16 * odd, 24)], mbuf.at[bands, 40:64],
-                ms_send.at[2, a], ms_recv.at[2, a], inner, c,
-            )
+            for level in range(3):
+                high, low = parts_of(z[:, 128 * level : 128 * level + 128])
+                for at, part in ((0, high), (1, low), (2, high)):
+                    first = PAN_EXT * at + rows
+                    zbuf[level, first : first + count, 128 * j : 128 * j + 128] = part
+
+    def ms_columns(bands, at):
+        high, low = parts_of(xbuf[0 : 32 * len(bands)])
+        y = jnp.dot(
+            jnp.concatenate([high, low, high], 1), ms_cols[...], preferred_element_type=jnp.float32
         )
-        inner_copies[-1].start()
-
-    for copy in pan_copies:
-        copy.wait_recv()
-    for step in range(0, PAN_EXT, 8):
-        rows = slice(step, step + 8)
-        if step < PAN_RIM:
-            base, at, count = 0, 64, 16
-        elif step < PAN_RIM + ROWS:
-            base, at, count = PAN_RIM, 0, 64
-        else:
-            base, at, count = PAN_RIM + ROWS, 80, 16
-        second = step - base >= count
-        inside = step - base - (count if second else 0)
-        left = precv[0, at + inside : at + inside + 8]
-        right = precv[1, at + inside : at + inside + 8]
-        if second:
-            left = pltpu.roll(left, 64, 1)
-        else:
-            right = pltpu.roll(right, 64, 1)
-        tiles = [left]
-        tiles += [pltpu.roll(pan_ext[rows, 128 * t : 128 * t + 128], 64, 1) for t in range(4)]
-        tiles += [right]
-        for t in range(5):
-            pan_roll[rows, 128 * t : 128 * t + 128] = jnp.where(lane < 64, tiles[t], tiles[t + 1])
-    pan_split[0], pan_split[1] = parts_of(pan_roll[...])
-
+        high, low = parts_of(y)
+        for i, b in enumerate(bands):
+            ysplit[b, at : at + 32] = high[32 * i : 32 * i + 32]
+            ysplit[b, 64 + at : 96 + at] = low[32 * i : 32 * i + 32]
+
+    for b in range(BANDS):
+        rim = mbuf[b, 16:24]
+        for q, first in enumerate((0, 8, 24, 32)):
+            rows = slice(32 * b + 8 * q, 32 * b + 8 * q + 8)
+            xbuf[rows, 0:128] = mbuf[b, first : first + 8]
+            xbuf[rows, 128:256] = pltpu.roll(rim, (128 - 32 * q) % 128, 1)
     for load in table_loads:
         load.wait()
-    for j in range(4):
-        window = slice(128 * j, 128 * j + 256)
-        high, low = pan_split[0, :, window], pan_split[1, :, window]
-        z = jnp.dot(
-            jnp.concatenate([high, low, high], 1), pan_cols[...], preferred_element_type=jnp.float32
-        )
-        for level in range(3):
-            high, low = parts_of(z[:, 128 * level : 128 * level + 128])
-            for at, part in ((0, high), (1, low), (2, high)):
-                zbuf[level, PAN_EXT * at : PAN_EXT * (at + 1), 128 * j : 128 * j + 128] = part
+    ms_columns(range(BANDS), 0)
+
+    remote(pstage, precv, send_sems.at[4], pan_recv.at[1], r, col_of[0, 1]).wait_recv()
+    tiles = [pan_own[:, 128 * t : 128 * t + 128] for t in range(4)]
+    pan_columns(0, ROWS, tiles, unpacked(precv))
+    remote(psums, psums, send_sems.at[3], pan_recv.at[0], row_of[1], c).wait_recv()
+    remote(cstage, crecv, send_sems.at[5], pan_recv.at[2], row_of[1], c).wait_recv()
+    tiles = [
+        jnp.concatenate([pan_above_below[way, :, 128 * t : 128 * t + 128] for way in range(2)], 0)
+        for t in range(4)
+    ]
+    ends = jnp.concatenate([unpacked(crecv.at[0]), unpacked(crecv.at[1])], 0)
+    pan_columns(ROWS, 2 * PAN_RIM, tiles, ends)
     for level in range(3):
         qbuf[level] = jnp.dot(pan_rows[level], zbuf[level], preferred_element_type=jnp.float32)
 
     def weigh(step, carry):
         rows = pl.ds(pl.multiple_of(8 * step, 8), 8)
-        own_rows = pl.ds(pl.multiple_of(8 * step + PAN_RIM, 8), 8)
-        fields = [pan_ext[own_rows, :]] + [qbuf[level, rows, :] for level in range(3)]
+        fields = [pan_own[rows, :]] + [qbuf[level, rows, :] for level in range(3)]
         for b in range(BANDS):
             g1, g2, g3 = gains[0, b], gains[1, b], gains[2, b]
             terms[b, rows, :] = (
@@ -432,22 +436,17 @@
     lax.fori_loop(0, ROWS // 8, weigh, 0)
 
     for a in range(2):
-        inner_copies[a].wait_recv()
-        for k in range(half):
-            sender = col_of[a, k]
-            remote(
-                ostage.at[sender], obuf.at[sender],
-                ms_send.at[1, half * a + k], ms_recv.at[1, sender], outer, sender,
-            ).wait_recv()
-        for k in range(half):
-            b = halves[a] + k
-            parts = [(mbuf[b, m : m + 8], mbuf[b, 16:24], 32 * q) for q, m in enumerate((0, 8, 24, 32))]
+        arrived = mbuf.at[0:half, 0:24]
+        remote(arrived, arrived, send_sems.at[2], ms_recv.at[2, a], inner, c).wait_recv()
+        arrived = obuf.at[0:half]
+        remote(arrived, arrived, send_sems.at[1], ms_recv.at[1, a], outer, c).wait_recv()
+        bands = [halves[a] + k for k in range(half)]
+        for k, b in enumerate(bands):
             rim = mbuf[b, rows_of(56 - 16 * odd, 8)]
             for q in range(2):
-                parts.append((mbuf[b, rows_of(40 + 8 * odd + 8 * q, 8)], rim, 32 * q + 64 * odd))
-            for g, (main, rim, at) in enumerate(parts):
-                rows = slice(64 * k + 8 * g, 64 * k + 8 * g + 8)
-                xbuf[rows, 0:128] = main
+                rows = slice(32 * k + 8 * q, 32 * k + 8 * q + 8)
+                xbuf[rows, 0:128] = mbuf[b, rows_of(40 + 8 * odd + 8 * q, 8)]
+                at = 32 * q + 64 * odd
                 xbuf[rows, 128:256] = pltpu.roll(rim, lax.rem(128 - at, 128), 1)
             upper, lower = obuf[b, 0:8], obuf[b, 8:16]
             rims = [upper, lower]
@@ -462,32 +461,23 @@
                             inside &= (lane >= first) & (lane < last)
                         rims[v] = jnp.where(inside, moved, rims[v])
             for v, main in enumerate((upper, lower)):
-                rows = slice(64 * k + 48 + 8 * v, 64 * k + 56 + 8 * v)
+                rows = slice(32 * k + 16 + 8 * v, 32 * k + 24 + 8 * v)
                 xbuf[rows, 0:128] = main
                 xbuf[rows, 128:256] = rims[v]
-        high, low = parts_of(xbuf[...])
-        y = jnp.dot(
-            jnp.concatenate([high, low, high], 1), ms_cols[...], preferred_element_type=jnp.float32
-        )
-        high, low = parts_of(y)
-        for k in range(half):
-            ysplit[halves[a] + k, 0:64] = high[64 * k : 64 * k + 64]
-            ysplit[halves[a] + k, 64:128] = low[64 * k : 64 * k + 64]
-
-    for copy in same_copies + pan_copies + outer_copies + inner_copies:
-        copy.wait_send()
-
-
-def finish(terms, ysplit, ms_rows, out_hbm, result, sems):
-    copies = []
+        ms_columns(bands, 32)
+
+    sent = (stage.at[0 : nc - 1], ostage, mbuf.at[:, 0:24], psums, pstage, cstage)
+    for at, source in enumerate(sent):
+        remote(source, source, send_sems.at[at], pan_recv.at[0], inner, c).wait_send()
+
+
+def finish(terms, ysplit, ms_rows, out_hbm, result, sem):
     for b in range(BANDS):
         high = ysplit[b, 0:64]
         column = jnp.concatenate([high, ysplit[b, 64:128], high], 0)
         result[b] = terms[b] + jnp.dot(ms_rows[...], column, preferred_element_type=jnp.float32)
-        copies.append(pltpu.make_async_copy(result.at[b], out_hbm.at[b], sems.at[b]))
-        copies[-1].start()
-    for copy in copies:
-        copy.wait()
+        pltpu.make_async_copy(result.at[b], out_hbm.at[b], sem).start()
+    pltpu.make_async_copy(result, out_hbm, sem).wait()
 
 
 def in_hbm(x):
@@ -514,23 +504,23 @@
             pltpu.VMEM((nc, 16, 128), f32),
             pltpu.VMEM((BANDS, 64, 128), f32),
             pltpu.VMEM((BANDS, 16, 128), f32),
-            pltpu.VMEM((PAN_EXT, COLS), f32),
+            pltpu.VMEM((ROWS, COLS), f32),
             pltpu.VMEM((2, PAN_RIM, COLS), f32),
-            pltpu.VMEM((2, 96, 128), f32),
-            pltpu.VMEM((2, 96, 128), f32),
+            pltpu.VMEM((2, PAN_RIM, COLS), f32),
+            pltpu.VMEM((2, 64, 128), f32),
+            pltpu.VMEM((2, 64, 128), f32),
+            pltpu.VMEM((2, 2, 16, 128), f32),
+            pltpu.VMEM((2, 2, 16, 128), f32),
             *[pltpu.VMEM(table.shape, bf16) for table in tables[1:]],
-            pltpu.VMEM((PAN_EXT, COLS + 128), f32),
             pltpu.VMEM((2, PAN_EXT, COLS + 128), bf16),
             pltpu.VMEM((3, 3 * PAN_EXT, COLS), bf16),
             pltpu.VMEM((3, ROWS, COLS), f32),
             pltpu.VMEM((BANDS * 32, 256), f32),
             pltpu.SMEM((3, BANDS), f32),
             pltpu.SemaphoreType.DMA((8,)),
-            pltpu.SemaphoreType.DMA,
-            pltpu.SemaphoreType.DMA((3, nc)),
-            pltpu.SemaphoreType.DMA((3, nc)),
-            pltpu.SemaphoreType.DMA((8,)),
-            pltpu.SemaphoreType.DMA((8,)),
+            pltpu.SemaphoreType.DMA((3, 2)),
+            pltpu.SemaphoreType.DMA((3,)),
+            pltpu.SemaphoreType.DMA((6,)),
         ],
         compiler_params=pltpu.CompilerParams(
             collective_id=0, has_side_effects=True, vmem_limit_bytes=32 * 1024 * 1024
@@ -541,7 +531,7 @@
         out_shape=jax.ShapeDtypeStruct((BANDS, ROWS, COLS), f32),
         in_specs=[vmem] * 3,
         out_specs=hbm,
-        scratch_shapes=[pltpu.VMEM((BANDS, ROWS, COLS), f32), pltpu.SemaphoreType.DMA((BANDS,))],
+        scratch_shapes=[pltpu.VMEM((BANDS, ROWS, COLS), f32), pltpu.SemaphoreType.DMA],
         compiler_params=pltpu.CompilerParams(vmem_limit_bytes=16 * 1024 * 1024),
     )(*shared)
 

time: 19.4 us -> 18.2 us (0.938)
  Pallas kernels: 19.2 us -> 18.1 us
    pallas_call x1, Pallas kernels: 17.7 us -> 16.6 us  [on_device(): pl.pallas_call(functools.partial(spread, nr, nc), out_shape=[pltpu.VMEM((...]
where the time goes in v5:
time: 18.2 us; the launch traced here: 18.1 us
  Pallas kernels  18.1 us (99%)
    pallas_call x1, Pallas kernels, on_device(): pl.pallas_call(functools.partial(spread, nr, nc), out_shape=[pltpu.VMEM((...  16.6 us
    pallas_call x1, Pallas kernels, on_device(): pl.pallas_call(finish, out_shape=jax.ShapeDtypeStruct((BANDS, ROWS, COLS)...  1.5 us

profile of v5, /device:TPU:0, one launch (start us, length us, event | category | flops | bytes accessed | tf_op | source)
XLA Modules:
  0.0 18.1 jit_solution(1912868268726493609)
XLA Ops:
  0.0 16.6 %shard_map.82 = (f32[8,128,512]{2,1,0:T(8,128)S(1)}, bf16[8,128,512]{2,1,0:T(8,128)(2,1)S(1)}, bf16[128,192]{1,0:T(8,128)(2,1)S(1)}) custom-call(f32[1,32,1024]{2,1,0:T(8,128)} %ms_hbm.1, f32[128,512]{1,0:T(8,128)} %pan_hbm.1, f32[3,8]{1,0:T(4,128)} %bitcast.1, bf16[2,128,192]{2,1,0:T(8,128)(2,1)} %constant.10.clone.ms_rows_hbm, ...), custom_call_target="tpu_custom_call" | custom-call | tf_op jit(solution)/shard_map/pallas_call | solution.py:492
  16.6 1.5 %shard_map.83 = f32[8,128,512]{2,1,0:T(8,128)} custom-call(f32[8,128,512]{2,1,0:T(8,128)S(1)} %get-tuple-element.8.terms, bf16[8,128,512]{2,1,0:T(8,128)(2,1)S(1)} %get-tuple-element.9.ysplit, bf16[128,192]{1,0:T(8,128)(2,1)S(1)} %get-tuple-element.10.ms_rows), custom_call_target="tpu_custom_call" | custom-call | tf_op jit(solution)/shard_map/pallas_call | solution.py:529

commit v6 on v5

--- a/solution.py
+++ b/solution.py
@@ -185,13 +185,21 @@
     return [jnp.where(left, one, two) for one, two in zip(firsts, seconds)]
 
 
+def column_parts(x, ms_cols):
+    high, low = parts_of(x)
+    y = jnp.dot(
+        jnp.concatenate([high, low, high], 1), ms_cols[...], preferred_element_type=jnp.float32
+    )
+    return parts_of(y)
+
+
 def spread(
     nr, nc,
     ms_hbm, pan_hbm, gains_hbm, ms_rows_hbm, ms_cols_hbm, pan_cols_hbm, pan_rows_hbm, sums_hbm,
-    terms, ysplit, ms_rows,
-    ms_own, stage, ostage, mbuf, obuf, pan_own, psums, pan_above_below, pstage, precv, cstage, crecv,
-    ms_cols, pan_cols, pan_rows, sums,
-    pan_split, zbuf, qbuf, xbuf,
+    pan_own, qbuf, weights, ysplit, xlast, ms_cols, ms_rows,
+    ms_own, stage, ostage, mbuf, obuf, psums, pan_above_below, pstage, precv, cstage, crecv,
+    pan_cols, pan_rows, sums,
+    pan_split, zbuf, xbuf,
     gains, load_sems, ms_recv, pan_recv, send_sems,
 ):
     r, c = lax.axis_index("row"), lax.axis_index("col")
@@ -390,11 +398,7 @@
                     zbuf[level, first : first + count, 128 * j : 128 * j + 128] = part
 
     def ms_columns(bands, at):
-        high, low = parts_of(xbuf[0 : 32 * len(bands)])
-        y = jnp.dot(
-            jnp.concatenate([high, low, high], 1), ms_cols[...], preferred_element_type=jnp.float32
-        )
-        high, low = parts_of(y)
+        high, low = column_parts(xbuf[0 : 32 * len(bands)], ms_cols)
         for i, b in enumerate(bands):
             ysplit[b, at : at + 32] = high[32 * i : 32 * i + 32]
             ysplit[b, 64 + at : 96 + at] = low[32 * i : 32 * i + 32]
@@ -423,17 +427,10 @@
     for level in range(3):
         qbuf[level] = jnp.dot(pan_rows[level], zbuf[level], preferred_element_type=jnp.float32)
 
-    def weigh(step, carry):
-        rows = pl.ds(pl.multiple_of(8 * step, 8), 8)
-        fields = [pan_own[rows, :]] + [qbuf[level, rows, :] for level in range(3)]
-        for b in range(BANDS):
-            g1, g2, g3 = gains[0, b], gains[1, b], gains[2, b]
-            terms[b, rows, :] = (
-                g1 * fields[0] + (g2 - g1) * fields[1] + (g3 - g2) * fields[2] - g3 * fields[3]
-            )
-        return carry
-
-    lax.fori_loop(0, ROWS // 8, weigh, 0)
+    for b in range(BANDS):
+        g1, g2, g3 = gains[0, b], gains[1, b], gains[2, b]
+        for at, weight in enumerate((g1, g2 - g1, g3 - g2, -g3)):
+            weights[4 * b + at : 4 * b + at + 1] = jnp.full((1, COLS), weight, jnp.float32)
 
     for a in range(2):
         arrived = mbuf.at[0:half, 0:24]
@@ -441,13 +438,14 @@
         arrived = obuf.at[0:half]
         remote(arrived, arrived, send_sems.at[1], ms_recv.at[1, a], outer, c).wait_recv()
         bands = [halves[a] + k for k in range(half)]
+        target = xlast if a else xbuf
         for k, b in enumerate(bands):
             rim = mbuf[b, rows_of(56 - 16 * odd, 8)]
             for q in range(2):
                 rows = slice(32 * k + 8 * q, 32 * k + 8 * q + 8)
-                xbuf[rows, 0:128] = mbuf[b, rows_of(40 + 8 * odd + 8 * q, 8)]
+                target[rows, 0:128] = mbuf[b, rows_of(40 + 8 * odd + 8 * q, 8)]
                 at = 32 * q + 64 * odd
-                xbuf[rows, 128:256] = pltpu.roll(rim, lax.rem(128 - at, 128), 1)
+                target[rows, 128:256] = pltpu.roll(rim, lax.rem(128 - at, 128), 1)
             upper, lower = obuf[b, 0:8], obuf[b, 8:16]
             rims = [upper, lower]
             for i, count, at, first, last in RIM_PIECES:
@@ -462,21 +460,40 @@
                         rims[v] = jnp.where(inside, moved, rims[v])
             for v, main in enumerate((upper, lower)):
                 rows = slice(32 * k + 16 + 8 * v, 32 * k + 24 + 8 * v)
-                xbuf[rows, 0:128] = main
-                xbuf[rows, 128:256] = rims[v]
-        ms_columns(bands, 32)
+                target[rows, 0:128] = main
+                target[rows, 128:256] = rims[v]
+        if a == 0:
+            ms_columns(bands, 32)
 
     sent = (stage.at[0 : nc - 1], ostage, mbuf.at[:, 0:24], psums, pstage, cstage)
     for at, source in enumerate(sent):
         remote(source, source, send_sems.at[at], pan_recv.at[0], inner, c).wait_send()
 
 
-def finish(terms, ysplit, ms_rows, out_hbm, result, sem):
-    for b in range(BANDS):
-        high = ysplit[b, 0:64]
-        column = jnp.concatenate([high, ysplit[b, 64:128], high], 0)
-        result[b] = terms[b] + jnp.dot(ms_rows[...], column, preferred_element_type=jnp.float32)
-        pltpu.make_async_copy(result.at[b], out_hbm.at[b], sem).start()
+def finish(nc, pan, qbuf, weights, ysplit, xlast, ms_cols, ms_rows, out_hbm, result, sem):
+    half = nc // 2
+    side = lax.axis_index("col") // half
+    for a in range(2):
+        first = lax.rem(side + a, 2) * half
+        if a:
+            rim_high, rim_low = column_parts(xlast[...], ms_cols)
+        for k in range(half):
+            b = first + k
+            if a:
+                rows = slice(32 * k, 32 * k + 32)
+                high = jnp.concatenate([ysplit[b, 0:32], rim_high[rows]], 0)
+                low = jnp.concatenate([ysplit[b, 64:96], rim_low[rows]], 0)
+            else:
+                high, low = ysplit[b, 0:64], ysplit[b, 64:128]
+            total = jnp.dot(
+                ms_rows[...],
+                jnp.concatenate([high, low, high], 0),
+                preferred_element_type=jnp.float32,
+            )
+            for at, field in enumerate((pan, qbuf.at[0], qbuf.at[1], qbuf.at[2])):
+                total += weights[pl.ds(4 * b + at, 1)] * field[...]
+            result[b] = total
+            pltpu.make_async_copy(result.at[b], out_hbm.at[b], sem).start()
     pltpu.make_async_copy(result, out_hbm, sem).wait()
 
 
@@ -492,29 +509,31 @@
     shared = pl.pallas_call(
         functools.partial(spread, nr, nc),
         out_shape=[
-            pltpu.VMEM((BANDS, ROWS, COLS), f32),
+            pltpu.VMEM((ROWS, COLS), f32),
+            pltpu.VMEM((3, ROWS, COLS), f32),
+            pltpu.VMEM((4 * BANDS, COLS), f32),
             pltpu.VMEM((BANDS, 128, COLS), bf16),
+            pltpu.VMEM((BANDS // 2 * 32, 256), f32),
+            pltpu.VMEM(tables[1].shape, bf16),
             pltpu.VMEM(tables[0].shape[1:], bf16),
         ],
         in_specs=[hbm] * 8,
-        out_specs=[vmem] * 3,
+        out_specs=[vmem] * 7,
         scratch_shapes=[
             pltpu.VMEM((LROWS, nc * LCOLS), f32),
             pltpu.VMEM((nc, 40, 128), f32),
             pltpu.VMEM((nc, 16, 128), f32),
             pltpu.VMEM((BANDS, 64, 128), f32),
             pltpu.VMEM((BANDS, 16, 128), f32),
-            pltpu.VMEM((ROWS, COLS), f32),
             pltpu.VMEM((2, PAN_RIM, COLS), f32),
             pltpu.VMEM((2, PAN_RIM, COLS), f32),
             pltpu.VMEM((2, 64, 128), f32),
             pltpu.VMEM((2, 64, 128), f32),
             pltpu.VMEM((2, 2, 16, 128), f32),
             pltpu.VMEM((2, 2, 16, 128), f32),
-            *[pltpu.VMEM(table.shape, bf16) for table in tables[1:]],
+            *[pltpu.VMEM(table.shape, bf16) for table in tables[2:]],
             pltpu.VMEM((2, PAN_EXT, COLS + 128), bf16),
             pltpu.VMEM((3, 3 * PAN_EXT, COLS), bf16),
-            pltpu.VMEM((3, ROWS, COLS), f32),
             pltpu.VMEM((BANDS * 32, 256), f32),
             pltpu.SMEM((3, BANDS), f32),
             pltpu.SemaphoreType.DMA((8,)),
@@ -527,9 +546,9 @@
         ),
     )(in_hbm(ms), in_hbm(pan), in_hbm(gains.T), *[in_hbm(jnp.asarray(table)) for table in tables])
     return pl.pallas_call(
-        finish,
+        functools.partial(finish, nc),
         out_shape=jax.ShapeDtypeStruct((BANDS, ROWS, COLS), f32),
-        in_specs=[vmem] * 3,
+        in_specs=[vmem] * 7,
         out_specs=hbm,
         scratch_shapes=[pltpu.VMEM((BANDS, ROWS, COLS), f32), pltpu.SemaphoreType.DMA],
         compiler_params=pltpu.CompilerParams(vmem_limit_bytes=16 * 1024 * 1024),

time: 18.2 us -> 17.8 us (0.978)
  Pallas kernels: 18.1 us -> 17.6 us
    pallas_call x1, Pallas kernels: 16.6 us -> 15.9 us  [on_device(): pl.pallas_call(functools.partial(spread, nr, nc), out_shape=[pltpu.VMEM((...]
    pallas_call x1, Pallas kernels: 1.5 us -> 1.77 us  [on_device(): pl.pallas_call(functools.partial(finish, nc), out_shape=jax.ShapeDtypeStr...]
where the time goes in v6:
time: 17.8 us; the launch traced here: 17.6 us
  Pallas kernels  17.6 us (99%)
    pallas_call x1, Pallas kernels, on_device(): pl.pallas_call(functools.partial(spread, nr, nc), out_shape=[pltpu.VMEM((...  15.9 us
    pallas_call x1, Pallas kernels, on_device(): pl.pallas_call(functools.partial(finish, nc), out_shape=jax.ShapeDtypeStr...  1.77 us

profile of v6, /device:TPU:0, one launch (start us, length us, event | category | flops | bytes accessed | tf_op | source)
XLA Modules:
  0.0 17.6 jit_solution(673785061199893555)
XLA Ops:
  0.0 15.9 %shard_map.82 = (f32[128,512]{1,0:T(8,128)S(1)}, f32[3,128,512]{2,1,0:T(8,128)S(1)}, f32[32,512]{1,0:T(8,128)S(1)}, bf16[8,128,512]{2,1,0:T(8,128)(2,1)S(1)}, f3...) custom-call(f32[1,32,1024]{2,1,0:T(8,128)} %ms_hbm.1, f32[128,512]{1,0:T(8,128)} %pan_hbm.1, ...), custom_call_target="tpu_custom_call" | custom-call | tf_op jit(solution)/shard_map/pallas_call | solution.py:509
  15.9 1.8 %shard_map.83 = f32[8,128,512]{2,1,0:T(8,128)} custom-call(f32[128,512]{1,0:T(8,128)S(1)} %get-tuple-element.12.pan, f32[3,128,512]{2,1,0:T(8,128)S(1)} %get-tuple-element.13.qbuf, f32[32,512]{1,0:T(8,128)S(1)} %get-tuple-element.14.weights, bf16[8,128,512]{2,1,0:T(8,128)(2,1)S(1)} %get-tuple-element.15.ysplit, f32[128,256]{1,0:T(8,128)S(1)} %get-tuple-element.16.xlast, ...), custom_call_target="tpu_custom_call" | custom-call | tf_op jit(solution)/shard_map/pallas_call | solution.py:548

commit v7 on v6

--- a/solution.py
+++ b/solution.py
@@ -196,8 +196,8 @@
 def spread(
     nr, nc,
     ms_hbm, pan_hbm, gains_hbm, ms_rows_hbm, ms_cols_hbm, pan_cols_hbm, pan_rows_hbm, sums_hbm,
-    pan_own, qbuf, weights, ysplit, xlast, ms_cols, ms_rows,
-    ms_own, stage, ostage, mbuf, obuf, psums, pan_above_below, pstage, precv, cstage, crecv,
+    details, weights, ysplit, xlast, ms_cols, ms_rows,
+    ms_own, stage, ostage, mbuf, obuf, pan_own, psums, pan_above_below, pstage, precv, cstage, crecv,
     pan_cols, pan_rows, sums,
     pan_split, zbuf, xbuf,
     gains, load_sems, ms_recv, pan_recv, send_sems,
@@ -214,9 +214,6 @@
     ms_load = pltpu.make_async_copy(ms_hbm.at[0], ms_own, load_sems.at[0])
     pan_load = pltpu.make_async_copy(pan_hbm, pan_own, load_sems.at[1])
     sums_load = pltpu.make_async_copy(sums_hbm, sums, load_sems.at[7])
-    ms_load.start()
-    pan_load.start()
-    sums_load.start()
 
     odd = lax.rem(r, 2)
     inner = lax.rem(r + 1 - 2 * odd + nr, nr)
@@ -233,6 +230,9 @@
             barrier, inc=1, device_id=(inner, lax.rem(c + k, nc)), device_id_type=MESH
         )
 
+    ms_load.start()
+    pan_load.start()
+    sums_load.start()
     table_loads = [
         pltpu.make_async_copy(source, target, load_sems.at[2 + i])
         for i, (source, target) in enumerate(
@@ -424,13 +424,16 @@
     ]
     ends = jnp.concatenate([unpacked(crecv.at[0]), unpacked(crecv.at[1])], 0)
     pan_columns(ROWS, 2 * PAN_RIM, tiles, ends)
+    finer = pan_own[...]
     for level in range(3):
-        qbuf[level] = jnp.dot(pan_rows[level], zbuf[level], preferred_element_type=jnp.float32)
+        coarser = jnp.dot(pan_rows[level], zbuf[level], preferred_element_type=jnp.float32)
+        details[level] = finer - coarser
+        finer = coarser
 
     for b in range(BANDS):
-        g1, g2, g3 = gains[0, b], gains[1, b], gains[2, b]
-        for at, weight in enumerate((g1, g2 - g1, g3 - g2, -g3)):
-            weights[4 * b + at : 4 * b + at + 1] = jnp.full((1, COLS), weight, jnp.float32)
+        for level in range(3):
+            at = 3 * b + level
+            weights[at : at + 1] = jnp.full((1, COLS), gains[level, b], jnp.float32)
 
     for a in range(2):
         arrived = mbuf.at[0:half, 0:24]
@@ -470,7 +473,7 @@
         remote(source, source, send_sems.at[at], pan_recv.at[0], inner, c).wait_send()
 
 
-def finish(nc, pan, qbuf, weights, ysplit, xlast, ms_cols, ms_rows, out_hbm, result, sem):
+def finish(nc, details, weights, ysplit, xlast, ms_cols, ms_rows, out_hbm, result, sem):
     half = nc // 2
     side = lax.axis_index("col") // half
     for a in range(2):
@@ -490,10 +493,12 @@
                 jnp.concatenate([high, low, high], 0),
                 preferred_element_type=jnp.float32,
             )
-            for at, field in enumerate((pan, qbuf.at[0], qbuf.at[1], qbuf.at[2])):
-                total += weights[pl.ds(4 * b + at, 1)] * field[...]
+            for level in range(3):
+                total += weights[pl.ds(3 * b + level, 1)] * details[level]
             result[b] = total
-            pltpu.make_async_copy(result.at[b], out_hbm.at[b], sem).start()
+            for part in range(2):
+                rows = pl.ds(64 * part, 64)
+                pltpu.make_async_copy(result.at[b, rows], out_hbm.at[b, rows], sem).start()
     pltpu.make_async_copy(result, out_hbm, sem).wait()
 
 
@@ -509,22 +514,22 @@
     shared = pl.pallas_call(
         functools.partial(spread, nr, nc),
         out_shape=[
-            pltpu.VMEM((ROWS, COLS), f32),
             pltpu.VMEM((3, ROWS, COLS), f32),
-            pltpu.VMEM((4 * BANDS, COLS), f32),
+            pltpu.VMEM((3 * BANDS, COLS), f32),
             pltpu.VMEM((BANDS, 128, COLS), bf16),
             pltpu.VMEM((BANDS // 2 * 32, 256), f32),
             pltpu.VMEM(tables[1].shape, bf16),
             pltpu.VMEM(tables[0].shape[1:], bf16),
         ],
         in_specs=[hbm] * 8,
-        out_specs=[vmem] * 7,
+        out_specs=[vmem] * 6,
         scratch_shapes=[
             pltpu.VMEM((LROWS, nc * LCOLS), f32),
             pltpu.VMEM((nc, 40, 128), f32),
             pltpu.VMEM((nc, 16, 128), f32),
             pltpu.VMEM((BANDS, 64, 128), f32),
             pltpu.VMEM((BANDS, 16, 128), f32),
+            pltpu.VMEM((ROWS, COLS), f32),
             pltpu.VMEM((2, PAN_RIM, COLS), f32),
             pltpu.VMEM((2, PAN_RIM, COLS), f32),
             pltpu.VMEM((2, 64, 128), f32),
@@ -548,7 +553,7 @@
     return pl.pallas_call(
         functools.partial(finish, nc),
         out_shape=jax.ShapeDtypeStruct((BANDS, ROWS, COLS), f32),
-        in_specs=[vmem] * 7,
+        in_specs=[vmem] * 6,
         out_specs=hbm,
         scratch_shapes=[pltpu.VMEM((BANDS, ROWS, COLS), f32), pltpu.SemaphoreType.DMA],
         compiler_params=pltpu.CompilerParams(vmem_limit_bytes=16 * 1024 * 1024),

time: 17.8 us -> 17.7 us (level)
  no operation moved by 1% of the time
where the time goes in v7:
time: 17.7 us; the launch traced here: 17.6 us
  Pallas kernels  17.5 us (99%)
    pallas_call x1, Pallas kernels, on_device(): pl.pallas_call(functools.partial(spread, nr, nc), out_shape=[pltpu.VMEM((...  15.8 us
    pallas_call x1, Pallas kernels, on_device(): pl.pallas_call(functools.partial(finish, nc), out_shape=jax.ShapeDtypeStr...  1.72 us

profile of v7, /device:TPU:0, one launch (start us, length us, event | category | flops | bytes accessed | tf_op | source)
XLA Modules:
  0.0 17.6 jit_solution(18429435755016466804)
XLA Ops:
  0.0 15.8 %shard_map.82 = (f32[3,128,512]{2,1,0:T(8,128)S(1)}, f32[24,512]{1,0:T(8,128)S(1)}, bf16[8,128,512]{2,1,0:T(8,128)(2,1)S(1)}, f32[128,256]{1,0:T(8,128)S(1)}, bf...) custom-call(f32[1,32,1024]{2,1,0:T(8,128)} %ms_hbm.1, f32[128,512]{1,0:T(8,128)} %pan_hbm.1, f32[3,8]{1,0:T(4,128)} %bitcast.1, ...), custom_call_target="tpu_custom_call" | custom-call | tf_op jit(solution)/shard_map/pallas_call | solution.py:514
  15.8 1.7 %shard_map.83 = f32[8,128,512]{2,1,0:T(8,128)} custom-call(f32[3,128,512]{2,1,0:T(8,128)S(1)} %get-tuple-element.11.details, f32[24,512]{1,0:T(8,128)S(1)} %get-tuple-element.12.weights, bf16[8,128,512]{2,1,0:T(8,128)(2,1)S(1)} %get-tuple-element.13.ysplit, f32[128,256]{1,0:T(8,128)S(1)} %get-tuple-element.14.xlast, ...), custom_call_target="tpu_custom_call" | custom-call | tf_op jit(solution)/shard_map/pallas_call | solution.py:553

commit v8 on v7

--- a/solution.py
+++ b/solution.py
@@ -476,29 +476,36 @@
 def finish(nc, details, weights, ysplit, xlast, ms_cols, ms_rows, out_hbm, result, sem):
     half = nc // 2
     side = lax.axis_index("col") // half
-    for a in range(2):
-        first = lax.rem(side + a, 2) * half
-        if a:
-            rim_high, rim_low = column_parts(xlast[...], ms_cols)
-        for k in range(half):
-            b = first + k
-            if a:
-                rows = slice(32 * k, 32 * k + 32)
-                high = jnp.concatenate([ysplit[b, 0:32], rim_high[rows]], 0)
-                low = jnp.concatenate([ysplit[b, 64:96], rim_low[rows]], 0)
-            else:
-                high, low = ysplit[b, 0:64], ysplit[b, 64:128]
-            total = jnp.dot(
-                ms_rows[...],
-                jnp.concatenate([high, low, high], 0),
-                preferred_element_type=jnp.float32,
-            )
-            for level in range(3):
-                total += weights[pl.ds(3 * b + level, 1)] * details[level]
-            result[b] = total
-            for part in range(2):
-                rows = pl.ds(64 * part, 64)
-                pltpu.make_async_copy(result.at[b, rows], out_hbm.at[b, rows], sem).start()
+    bands = [lax.rem(side + a, 2) * half + k for a in range(2) for k in range(half)]
+
+    def product(i, rims):
+        b = bands[i]
+        if i < half:
+            high, low = ysplit[b, 0:64], ysplit[b, 64:128]
+        else:
+            rows = slice(32 * (i - half), 32 * (i - half) + 32)
+            high = jnp.concatenate([ysplit[b, 0:32], rims[0][rows]], 0)
+            low = jnp.concatenate([ysplit[b, 64:96], rims[1][rows]], 0)
+        return jnp.dot(
+            ms_rows[...],
+            jnp.concatenate([high, low, high], 0),
+            preferred_element_type=jnp.float32,
+        )
+
+    rims = None
+    following = None
+    for i, b in enumerate(bands):
+        total = product(i, rims) if following is None else following
+        if i == half - 2:
+            rims = column_parts(xlast[...], ms_cols)
+        if 0 < i < BANDS - 1:
+            following = product(i + 1, rims)
+        for level in range(3):
+            total += weights[pl.ds(3 * b + level, 1)] * details[level]
+        result[b] = total
+        for part in range(2):
+            rows = pl.ds(64 * part, 64)
+            pltpu.make_async_copy(result.at[b, rows], out_hbm.at[b, rows], sem).start()
     pltpu.make_async_copy(result, out_hbm, sem).wait()
 
 

time: 17.7 us -> 17.6 us (level)
  no operation moved by 1% of the time
where the time goes in v8:
time: 17.6 us; the launch traced here: 17.5 us
  Pallas kernels  17.5 us (99%)
    pallas_call x1, Pallas kernels, on_device(): pl.pallas_call(functools.partial(spread, nr, nc), out_shape=[pltpu.VMEM((...  15.8 us
    pallas_call x1, Pallas kernels, on_device(): pl.pallas_call(functools.partial(finish, nc), out_shape=jax.ShapeDtypeStr...  1.65 us

profile of v8, /device:TPU:0, one launch (start us, length us, event | category | flops | bytes accessed | tf_op | source)
XLA Modules:
  0.0 17.5 jit_solution(11627950794205204396)
XLA Ops:
  0.0 15.8 %shard_map.82 = (f32[3,128,512]{2,1,0:T(8,128)S(1)}, f32[24,512]{1,0:T(8,128)S(1)}, bf16[8,128,512]{2,1,0:T(8,128)(2,1)S(1)}, f32[128,256]{1,0:T(8,128)S(1)}, bf...) custom-call(f32[1,32,1024]{2,1,0:T(8,128)} %ms_hbm.1, f32[128,512]{1,0:T(8,128)} %pan_hbm.1, f32[3,8]{1,0:T(4,128)} %bitcast.1, ...), custom_call_target="tpu_custom_call" | custom-call | tf_op jit(solution)/shard_map/pallas_call | solution.py:521
  15.8 1.7 %shard_map.83 = f32[8,128,512]{2,1,0:T(8,128)} custom-call(f32[3,128,512]{2,1,0:T(8,128)S(1)} %get-tuple-element.11.details, f32[24,512]{1,0:T(8,128)S(1)} %get-tuple-element.12.weights, bf16[8,128,512]{2,1,0:T(8,128)(2,1)S(1)} %get-tuple-element.13.ysplit, f32[128,256]{1,0:T(8,128)S(1)} %get-tuple-element.14.xlast, ...), custom_call_target="tpu_custom_call" | custom-call | tf_op jit(solution)/shard_map/pallas_call | solution.py:560

commit v9 on v8

--- a/solution.py
+++ b/solution.py
@@ -345,17 +345,17 @@
     for way, d in ((0, 1), (1, -1)):
         remote(
             psums.at[way], pan_above_below.at[way],
-            send_sems.at[3], pan_recv.at[0], row_of[d], c,
+            send_sems.at[1], pan_recv.at[0], row_of[d], c,
         ).start()
     for side_at, k in ((0, 1), (1, nc - 1)):
         beside = lax.rem(c + k, nc)
         remote(
-            pstage.at[side_at], precv.at[side_at], send_sems.at[4], pan_recv.at[1], r, beside
+            pstage.at[side_at], precv.at[side_at], send_sems.at[1], pan_recv.at[1], r, beside
         ).start()
         for way, d in ((0, 1), (1, -1)):
             remote(
                 cstage.at[way, side_at], crecv.at[way, side_at],
-                send_sems.at[5], pan_recv.at[2], row_of[d], beside,
+                send_sems.at[2], pan_recv.at[0], row_of[d], beside,
             ).start()
     send_outer(0)
 
@@ -413,11 +413,11 @@
         load.wait()
     ms_columns(range(BANDS), 0)
 
-    remote(pstage, precv, send_sems.at[4], pan_recv.at[1], r, col_of[0, 1]).wait_recv()
+    remote(pstage, precv, send_sems.at[1], pan_recv.at[1], r, col_of[0, 1]).wait_recv()
     tiles = [pan_own[:, 128 * t : 128 * t + 128] for t in range(4)]
     pan_columns(0, ROWS, tiles, unpacked(precv))
-    remote(psums, psums, send_sems.at[3], pan_recv.at[0], row_of[1], c).wait_recv()
-    remote(cstage, crecv, send_sems.at[5], pan_recv.at[2], row_of[1], c).wait_recv()
+    arrived = mbuf.at[:, 0:40]
+    remote(arrived, arrived, send_sems.at[1], pan_recv.at[0], row_of[1], c).wait_recv()
     tiles = [
         jnp.concatenate([pan_above_below[way, :, 128 * t : 128 * t + 128] for way in range(2)], 0)
         for t in range(4)
@@ -468,7 +468,7 @@
         if a == 0:
             ms_columns(bands, 32)
 
-    sent = (stage.at[0 : nc - 1], ostage, mbuf.at[:, 0:24], psums, pstage, cstage)
+    sent = (stage.at[0 : nc - 1], pan_own, psums)
     for at, source in enumerate(sent):
         remote(source, source, send_sems.at[at], pan_recv.at[0], inner, c).wait_send()
 
@@ -550,8 +550,8 @@
             pltpu.SMEM((3, BANDS), f32),
             pltpu.SemaphoreType.DMA((8,)),
             pltpu.SemaphoreType.DMA((3, 2)),
+            pltpu.SemaphoreType.DMA((2,)),
             pltpu.SemaphoreType.DMA((3,)),
-            pltpu.SemaphoreType.DMA((6,)),
         ],
         compiler_params=pltpu.CompilerParams(
             collective_id=0, has_side_effects=True, vmem_limit_bytes=32 * 1024 * 1024

time: 17.6 us -> 17.6 us (level)
  no operation moved by 1% of the time
where the time goes in v9:
time: 17.6 us; the launch traced here: 17.5 us
  Pallas kernels  17.4 us (99%)
    pallas_call x1, Pallas kernels, on_device(): pl.pallas_call(functools.partial(spread, nr, nc), out_shape=[pltpu.VMEM((...  15.8 us
    pallas_call x1, Pallas kernels, on_device(): pl.pallas_call(functools.partial(finish, nc), out_shape=jax.ShapeDtypeStr...  1.66 us

profile of v9, /device:TPU:0, one launch (start us, length us, event | category | flops | bytes accessed | tf_op | source)
XLA Modules:
  0.0 17.5 jit_solution(8067824255583827982)
XLA Ops:
  0.0 15.8 %shard_map.82 = (f32[3,128,512]{2,1,0:T(8,128)S(1)}, f32[24,512]{1,0:T(8,128)S(1)}, bf16[8,128,512]{2,1,0:T(8,128)(2,1)S(1)}, f32[128,256]{1,0:T(8,128)S(1)}, bf...) custom-call(f32[1,32,1024]{2,1,0:T(8,128)} %ms_hbm.1, f32[128,512]{1,0:T(8,128)} %pan_hbm.1, f32[3,8]{1,0:T(4,128)} %bitcast.1, ...), custom_call_target="tpu_custom_call" | custom-call | tf_op jit(solution)/shard_map/pallas_call | solution.py:521
  15.8 1.7 %shard_map.83 = f32[8,128,512]{2,1,0:T(8,128)} custom-call(f32[3,128,512]{2,1,0:T(8,128)S(1)} %get-tuple-element.11.details, f32[24,512]{1,0:T(8,128)S(1)} %get-tuple-element.12.weights, bf16[8,128,512]{2,1,0:T(8,128)(2,1)S(1)} %get-tuple-element.13.ysplit, f32[128,256]{1,0:T(8,128)S(1)} %get-tuple-element.14.xlast, ...), custom_call_target="tpu_custom_call" | custom-call | tf_op jit(solution)/shard_map/pallas_call | solution.py:560
